TPU v7x, 512 devices: a whole 4x8x8 slice. The times are simulated.
512 devices in a mesh: frame: 64 (over x, y, core), space: 8 (over z).
Axes of the slice: x: 4, y: 8, z: 8, core: 2. Of those that a mesh axis runs over, the one named last changes fastest.
Arguments:
- queries: bfloat16 [64, 256, 3072], P('frame', 'space'), may hold values from -8 to 8
- keys: bfloat16 [64, 256, 3072], P('frame', 'space'), may hold values from -8 to 8
- values: bfloat16 [64, 256, 3072], P('frame', 'space'), may hold values from -6 to 6
- windows: int32 [64, 8], P('frame'), may hold values from 1 to 16, as said below
Outputs:
- attended: bfloat16 [64, 256, 3072], P('frame', 'space')
Inputs may be any that keep to these rules, and one draw needn't show every extreme that they name: `windows`: column 2k and column 2k + 1 lie between max(1, 32 // 2^(k+2)) and 32 // 2^(k+1), and each column reaches its upper end at some frame.
All inputs are finite; a program needn't handle non-finite values.
Results may differ from a plain program's by a relative error of at most 0.006.
Values may be sent and summed in bfloat16 or wider, within the bound.
No kernel may reach another device: no remote copies, remote signals or barrier semaphores. Data moves between devices by JAX's collectives and lax.ppermute only.
A program may use at most 128 MiB of HBM per device.

v0:
```python
import math

import jax
import jax.numpy as jnp
from jax import lax
from jax.sharding import PartitionSpec as P

HD = 128
OCTAVES = 4


neg_large = -1e30


def extended(block, sides, width):
    for axis, dim in sides:
        count = lax.axis_size(axis)
        forward = [(i, i + 1) for i in range(count - 1)]
        backward = [(target, source) for source, target in forward]
        low = lax.ppermute(
            lax.slice_in_dim(block, block.shape[dim] - width, None, axis=dim), axis, forward
        )
        high = lax.ppermute(lax.slice_in_dim(block, 0, width, axis=dim), axis, backward)
        block = jnp.concatenate([low, block, high], axis=dim)
    return block


def shifted(array, axis, by):
    length = lax.axis_size(axis)
    pairs = [(i, i + by) for i in range(length) if 0 <= i + by < length]
    return lax.ppermute(array, axis, pairs)


def absorb(running, key_values, query_heads, key_mask, score_scale):
    row_max, denominator, accumulated = running
    key_count = key_values.shape[1]
    head_count = query_heads.shape[1]
    key_heads = key_values[0].reshape(key_count, head_count, HD)
    value_heads = key_values[1].reshape(key_count, head_count, HD)
    scores = (
        jnp.einsum("rhd,nhd->hrn", query_heads, key_heads, preferred_element_type=jnp.float32)
        * score_scale
    )
    if key_mask is not None:
        scores = jnp.where(key_mask[None], scores, neg_large)
    new_max = jnp.maximum(row_max, jnp.max(scores, axis=-1))
    shrink = jnp.exp(row_max - new_max)
    weights = jnp.exp(scores - new_max[:, :, None])
    if key_mask is not None:
        weights = jnp.where(key_mask[None], weights, 0.0)
    denominator = denominator * shrink + jnp.sum(weights, axis=-1)
    product = jnp.einsum(
        "hrn,nhd->hrd",
        weights.astype(jnp.bfloat16),
        value_heads,
        preferred_element_type=jnp.float32,
    )
    accumulated = accumulated * shrink[:, :, None] + product
    return (new_max, denominator, accumulated)


def trim_rims(key_block, rim_now, rim_keep):
    removed = rim_now - rim_keep
    return key_block[:, removed : key_block.shape[1] - removed]


def rows_plan(queries, keys, values, windows, score_scale):
    row_count = queries.shape[1]
    feat_width = queries.shape[2]
    head_count = feat_width // HD
    frame_pos = lax.axis_index("frame")
    frame_count = lax.axis_size("frame")
    space_pos = lax.axis_index("space")
    frame_rows = row_count * lax.axis_size("space")
    query_heads = queries[0].reshape(row_count, head_count, HD)
    own_pairs = jnp.stack([keys[0], values[0]])
    query_index = space_pos * row_count + jnp.arange(row_count, dtype=jnp.int32)
    running = (
        jnp.full((head_count, row_count), neg_large, jnp.float32),
        jnp.zeros((head_count, row_count), jnp.float32),
        jnp.zeros((head_count, row_count, HD), jnp.float32),
    )
    running = absorb(
        running,
        lax.all_gather(own_pairs, "space", axis=1, tiled=True),
        query_heads,
        None,
        score_scale,
    )
    widest = row_count // 2
    source = extended(own_pairs, (("space", 1),), widest)
    key_blocks = []
    key_masks = []
    for octave in range(OCTAVES):
        rim_width = row_count // 2 ** (octave + 1)
        keep_width = min(widest, rim_width)
        distance = 2**octave
        outgoing = trim_rims(source, widest, keep_width)
        got_below = shifted(outgoing, "frame", distance)
        got_above = shifted(outgoing, "frame", -distance)
        key_index = (
            space_pos * row_count
            - rim_width
            + jnp.arange(row_count + 2 * rim_width, dtype=jnp.int32)
        )
        in_frame = (key_index >= 0) & (key_index < frame_rows)
        row_gap = jnp.abs(query_index[:, None] - key_index[None, :])
        for column, partner, partner_keys in (
            (2 * octave, frame_pos - distance, got_below),
            (2 * octave + 1, frame_pos + distance, got_above),
        ):
            present = (partner >= 0) & (partner < frame_count)
            key_masks.append((row_gap <= windows[0, column]) & in_frame[None, :] & present)
            key_blocks.append(partner_keys)
    running = absorb(
        running,
        jnp.concatenate(key_blocks, 1),
        query_heads,
        jnp.concatenate(key_masks, 1),
        score_scale,
    )
    row_max, denominator, accumulated = running
    result = accumulated / denominator[:, :, None]
    return jnp.transpose(result, (1, 0, 2)).reshape(1, row_count, feat_width).astype(jnp.bfloat16)


def shards(queries, keys, values, windows):
    score_scale = 1.0 / math.sqrt(HD)
    attended = rows_plan(queries, keys, values, windows, score_scale)
    return attended


def solution(mesh):
    return jax.shard_map(
        shards,
        mesh=mesh,
        in_specs=(
            P("frame", "space", None),
            P("frame", "space", None),
            P("frame", "space", None),
            P("frame", None),
        ),
        out_specs=P("frame", "space", None),
        check_vma=False,
    )
```

profile of v0, /device:TPU:200, one launch (start us, length us, event | category | flops | bytes accessed | tf_op | source)
XLA Modules:
  0.0 198.6 jit_solution(9327757526744609202)
XLA Ops:
  6.5 1.0 constant_dynamic-update-slice_fusion.1
  7.5 0.9 constant_dynamic-update-slice_fusion
  8.4 1.2 copy.16
  9.7 5.5 %collective-permute-start = (bf16[2,16,3072]{2,1,0:T(8,128)(2,1)S(1)}, bf16[2,16,3072]{2,1,0:T(8,128)(2,1)S(1)}, u32[]{:S(2)}, u32[]{:S(2)}) collective-permute-start(bf16[2,16,3072]{2,1,0:T(8,128)(2,1)S(1)} %get-tuple-element.11), channel_id=1, source_target_pairs={{0,1},{1,2},{2,3},{3,4},{4,5},{5,6},{6,7},{8,9},{9,10},{10,11},{11... | collective-permute-start | bytes 589832 | tf_op jit(solution)/shard_map/ppermute | solution.py:20
  15.2 1.9 collective-permute-start.1
  17.2 0.7 fusion.54
  17.9 1.4 fusion.43
  19.2 0.1 collective-permute-done
  19.3 5.3 %collective-permute-done.1 = bf16[2,16,3072]{2,1,0:T(8,128)(2,1)S(1)} collective-permute-done((bf16[2,16,3072]{2,1,0:T(8,128)(2,1)S(1)}, bf16[2,16,3072]{2,1,0:T(8,128)(2,1)S(1)}, u32[]{:S(2)}, u32[]{:S(2)}) %collective-permute-start.1) | collective-permute-done | bytes 196640 | tf_op jit(solution)/shard_map/ppermute | solution.py:23
  24.7 0.1 slice.74
  24.8 1.2 copy.22
  26.1 6.8 %collective-permute-start.8 = (bf16[2,36,3072]{2,0,1:T(2,128)(2,1)}, bf16[2,36,3072]{2,0,1:T(2,128)(2,1)S(1)}, u32[]{:S(2)}, u32[]{:S(2)}) collective-permute-start(bf16[2,36,3072]{2,0,1:T(2,128)(2,1)} %copy.22), channel_id=1, source_target_pairs={{0,64},{8,72},{16,80},{24,88},{32,96},{40,104},{48,112},{56,120},{... | collective-permute-start | bytes 1327112 | tf_op jit(solution)/shard_map/ppermute | solution.py:31
  32.9 1.3 collective-permute-start.9
  34.2 0.9 slice.73
  35.1 2.7 %collective-permute-start.6 = (bf16[2,40,3072]{2,1,0:T(8,128)(2,1)}, bf16[2,40,3072]{2,1,0:T(8,128)(2,1)S(1)}, u32[]{:S(2)}, u32[]{:S(2)}) collective-permute-start(bf16[2,40,3072]{2,1,0:T(8,128)(2,1)} %slice.73), channel_id=1, source_target_pairs={{0,32},{8,40},{16,48},{24,56},{32,64},{40,72},{48,80},{56,88},{64,... | collective-permute-start | bytes 1474568 | tf_op jit(solution)/shard_map/ppermute | solution.py:31
  37.9 1.3 fusion.39
  39.2 1.9 collective-permute-start.2
  41.1 3.6 %collective-permute-start.3 = (bf16[2,64,3072]{2,1,0:T(8,128)(2,1)S(1)}, bf16[2,64,3072]{2,1,0:T(8,128)(2,1)}, u32[]{:S(2)}, u32[]{:S(2)}) collective-permute-start(bf16[2,64,3072]{2,1,0:T(8,128)(2,1)S(1)} %pad_maximum_fusion), channel_id=1, source_target_pairs={{8,0},{16,8},{24,16},{32,24},{40,32},{48,40},{56,48},{64,56},{72,6... | collective-permute-start | bytes 2359304 | tf_op jit(solution)/shard_map/ppermute | solution.py:31
  44.8 0.9 slice.72
  45.7 4.6 %collective-permute-done.8 = bf16[2,36,3072]{2,0,1:T(2,128)(2,1)S(1)} collective-permute-done((bf16[2,36,3072]{2,0,1:T(2,128)(2,1)}, bf16[2,36,3072]{2,0,1:T(2,128)(2,1)S(1)}, u32[]{:S(2)}, u32[]{:S(2)}) %collective-permute-start.8) | collective-permute-done | bytes 442400 | tf_op jit(solution)/shard_map/ppermute | solution.py:31
  50.3 5.0 %collective-permute-start.4 = (bf16[2,48,3072]{2,1,0:T(8,128)(2,1)}, bf16[2,48,3072]{2,1,0:T(8,128)(2,1)S(1)}, u32[]{:S(2)}, u32[]{:S(2)}) collective-permute-start(bf16[2,48,3072]{2,1,0:T(8,128)(2,1)} %slice.72), channel_id=1, source_target_pairs={{0,16},{8,24},{16,32},{24,40},{32,48},{40,56},{48,64},{56,72},{64,... | collective-permute-start | bytes 1769480 | tf_op jit(solution)/shard_map/ppermute | solution.py:31
  55.2 17.1 %collective-permute-done.9 = bf16[2,36,3072]{2,0,1:T(2,128)(2,1)} collective-permute-done((bf16[2,36,3072]{2,0,1:T(2,128)(2,1)}, bf16[2,36,3072]{2,0,1:T(2,128)(2,1)}, u32[]{:S(2)}, u32[]{:S(2)}) %collective-permute-start.9) | collective-permute-done | bytes 442400 | tf_op jit(solution)/shard_map/ppermute | solution.py:31
  72.4 1.9 collective-permute-start.5
  74.3 1.0 collective-permute-done.6
  75.3 1.3 collective-permute-start.7
  76.7 1.3 fusion.35
  78.0 1.4 fusion.31
  79.4 0.1 concatenate.9
  79.5 0.1 copy.24
  79.6 1.1 copy.25
  80.7 41.5 %collective-permute-done.7 = bf16[2,40,3072]{2,1,0:T(8,128)(2,1)} collective-permute-done((bf16[2,40,3072]{2,1,0:T(8,128)(2,1)}, bf16[2,40,3072]{2,1,0:T(8,128)(2,1)}, u32[]{:S(2)}, u32[]{:S(2)}) %collective-permute-start.7) | collective-permute-done | bytes 491552 | tf_op jit(solution)/shard_map/ppermute | solution.py:31
  122.2 24.3 %concatenate.11 = bf16[2,376,3072]{2,1,0:T(8,128)(2,1)} concatenate(bf16[2,64,3072]{2,1,0:T(8,128)(2,1)S(1)} %collective-permute-done.2, bf16[2,64,3072]{2,1,0:T(8,128)(2,1)} %collective-permute-done.3, bf16[2,48,3072]{2,1,0:T(8,128)(2,1)S(1)} %collective-permute-done.4, bf16[2,48,3072]{2,1,0:T(8,128)(2,1)} %collective-permute-done.5, bf16[2,40,3072]{2,1,0:T(8,128)(2,1)} %copy-done.2, ...), dimensions={1} | concatenate | bytes 9240576 | tf_op jit(solution)/shard_map/concatenate | solution.py:117
  146.5 4.7 %fusion.51 = (bf16[1,376,3072]{2,1,0:T(8,128)(2,1)}, bf16[1,376,3072]{2,1,0:T(8,128)(2,1)}) fusion(bf16[2,376,3072]{2,1,0:T(8,128)(2,1)} %concatenate.11), kind=kLoop, calls=%fused_computation.75 | loop fusion | bytes 9240576 | tf_op jit(solution)/shard_map/slice | solution.py:38
  151.2 3.0 %copy.26 = bf16[1,376,3072]{1,2,0:T(8,128)(2,1)S(1)} copy(bf16[1,376,3072]{2,1,0:T(8,128)(2,1)} %get-tuple-element.7) | data formatting | bytes 4620288 | tf_op jit(solution)/shard_map/slice | solution.py:38
  154.2 4.3 %copy.29 = bf16[1,376,3072]{1,2,0:T(8,128)(2,1)} copy(bf16[1,376,3072]{2,1,0:T(8,128)(2,1)} %get-tuple-element.8) | data formatting | bytes 4620288 | tf_op jit(solution)/shard_map/slice | solution.py:39
  158.5 1.6 fusion.56
  160.0 8.7 %fusion.52 = (bf16[1,256,3072]{2,0,1:T(2,128)(2,1)S(1)}, bf16[1,256,3072]{2,0,1:T(2,128)(2,1)}) fusion(bf16[2,256,3072]{2,0,1:T(2,128)(2,1)} %all-gather.2.cloned.1.call-done), kind=kLoop, calls=%fused_computation.76 | loop fusion | bytes 6291456 | tf_op jit(solution)/shard_map/slice | solution.py:39
  168.7 7.3 %copy.36 = bf16[1,256,3072]{1,2,0:T(8,128)(2,1)} copy(bf16[1,256,3072]{2,0,1:T(2,128)(2,1)} %get-tuple-element.10) | data formatting | bytes 3145728
  176.0 2.8 %fusion.55 = (f32[24,32]{1,0:T(8,128)S(1)}, f32[24,32,256]{2,1,0:T(8,128)}) fusion(bf16[256,24,128]{0,2,1:T(8,128)(2,1)} %bitcast.62, bf16[32,24,128]{2,1,0:T(8,128)(2,1)S(1)} %bitcast.64), kind=kOutput, calls=%fused_computation.79 | convolution fusion | flops 50724096 | bytes 2558976 | tf_op jit(solution)/shard_map/rhd,nhd->hrn/dot_general | solution.py:41
  178.8 0.6 broadcast_maximum_fusion
  179.4 1.0 fusion.8
  180.5 1.0 convolution_bitcast_fusion.1
  181.4 4.9 %copy.37 = bf16[1,256,3072]{1,2,0:T(8,128)(2,1)} copy(bf16[1,256,3072]{2,0,1:T(2,128)(2,1)S(1)} %get-tuple-element.9) | data formatting | bytes 3145728
  186.3 1.5 fusion.10
  187.8 0.7 bitcast_add_fusion
  188.5 2.4 %fusion.7 = bf16[32,24,128]{2,0,1:T(8,128)(2,1)S(1)} fusion(f32[32,24,128]{2,0,1:T(8,128)S(1)} %convolution_bitcast_fusion.1, bf16[256,24,128]{0,2,1:T(8,128)(2,1)} %bitcast.65, f32[24,32,256]{2,1,0:T(8,128)} %get-tuple-element.33, f32[24,32]{1,0:T(8,128)} %get-tuple-element.14, f32[32,24]{0,1:T(8,128)S(1)} %get-tuple-element.5, ...), kind=kOutput, calls=%fused_computation.12 | convolution fusion | flops 51216384 | bytes 2961408 | tf_op jit(solution)/shard_map/hrn,nhd->hrd/dot_general | solution.py:52
  190.9 0.1 copy.31
  191.0 0.8 convert_element_type.23
  (35 shorter events, 0.2 us)
Async XLA Ops:
  6.5 10.7 %copy-start.7 = (s32[1,8]{1,0:T(1,128)S(1)}, s32[1,8]{1,0:T(1,128)}, u32[]{:S(2)}) copy-start(s32[1,8]{1,0:T(1,128)} %param.7) | copy-start | bytes 100
  6.5 153.5 %all-gather.2.cloned.1.call-start = ((), (), s32[]{:S(2)}) async-start(), calls=%async_computation | async-start | bytes 3538944 | tf_op jit(solution)/shard_map/all_gather | solution.py:85
  9.7 9.6 %collective-permute-start = (bf16[2,16,3072]{2,1,0:T(8,128)(2,1)S(1)}, bf16[2,16,3072]{2,1,0:T(8,128)(2,1)S(1)}, u32[]{:S(2)}, u32[]{:S(2)}) collective-permute-start(bf16[2,16,3072]{2,1,0:T(8,128)(2,1)S(1)} %get-tuple-element.11), channel_id=1, source_target_pairs={{0,1},{1,2},{2,3},{3,4},{4,5},{5,6},{6,7},{8,9},{9,10},{10,11},{11... | collective-permute-start | bytes 589832 | tf_op jit(solution)/shard_map/ppermute | solution.py:20
  15.2 9.5 %collective-permute-start.1 = (bf16[2,16,3072]{2,1,0:T(8,128)(2,1)S(1)}, bf16[2,16,3072]{2,1,0:T(8,128)(2,1)S(1)}, u32[]{:S(2)}, u32[]{:S(2)}) collective-permute-start(bf16[2,16,3072]{2,1,0:T(8,128)(2,1)S(1)} %get-tuple-element.12), channel_id=1, source_target_pairs={{1,0},{2,1},{3,2},{4,3},{5,4},{6,5},{7,6},{9,8},{10,9},{11,10},{12... | collective-permute-start | bytes 589832 | tf_op jit(solution)/shard_map/ppermute | solution.py:23
  24.8 51.8 %copy-start.3 = (bf16[1,32,3072]{2,1,0:T(8,128)(2,1)S(1)}, bf16[1,32,3072]{2,1,0:T(8,128)(2,1)}, u32[]{:S(2)}) copy-start(bf16[1,32,3072]{2,1,0:T(8,128)(2,1)} %param.4) | copy-start | bytes 589828
  26.1 24.2 %collective-permute-start.8 = (bf16[2,36,3072]{2,0,1:T(2,128)(2,1)}, bf16[2,36,3072]{2,0,1:T(2,128)(2,1)S(1)}, u32[]{:S(2)}, u32[]{:S(2)}) collective-permute-start(bf16[2,36,3072]{2,0,1:T(2,128)(2,1)} %copy.22), channel_id=1, source_target_pairs={{0,64},{8,72},{16,80},{24,88},{32,96},{40,104},{48,112},{56,120},{... | collective-permute-start | bytes 1327112 | tf_op jit(solution)/shard_map/ppermute | solution.py:31
  32.9 39.4 %collective-permute-start.9 = (bf16[2,36,3072]{2,0,1:T(2,128)(2,1)}, bf16[2,36,3072]{2,0,1:T(2,128)(2,1)}, u32[]{:S(2)}, u32[]{:S(2)}) collective-permute-start(bf16[2,36,3072]{2,0,1:T(2,128)(2,1)} %copy.22), channel_id=1, source_target_pairs={{64,0},{72,8},{80,16},{88,24},{96,32},{104,40},{112,48},{120,56},{... | collective-permute-start | bytes 1327112 | tf_op jit(solution)/shard_map/ppermute | solution.py:31
  35.1 40.2 %collective-permute-start.6 = (bf16[2,40,3072]{2,1,0:T(8,128)(2,1)}, bf16[2,40,3072]{2,1,0:T(8,128)(2,1)S(1)}, u32[]{:S(2)}, u32[]{:S(2)}) collective-permute-start(bf16[2,40,3072]{2,1,0:T(8,128)(2,1)} %slice.73), channel_id=1, source_target_pairs={{0,32},{8,40},{16,48},{24,56},{32,64},{40,72},{48,80},{56,88},{64,... | collective-permute-start | bytes 1474568 | tf_op jit(solution)/shard_map/ppermute | solution.py:31
  39.2 82.9 %collective-permute-start.2 = (bf16[2,64,3072]{2,1,0:T(8,128)(2,1)S(1)}, bf16[2,64,3072]{2,1,0:T(8,128)(2,1)S(1)}, u32[]{:S(2)}, u32[]{:S(2)}) collective-permute-start(bf16[2,64,3072]{2,1,0:T(8,128)(2,1)S(1)} %pad_maximum_fusion), channel_id=1, source_target_pairs={{0,8},{8,16},{16,24},{24,32},{32,40},{40,48},{48,56},{56,64},{64,7... | collective-permute-start | bytes 2359304 | tf_op jit(solution)/shard_map/ppermute | solution.py:31
  41.1 81.0 %collective-permute-start.3 = (bf16[2,64,3072]{2,1,0:T(8,128)(2,1)S(1)}, bf16[2,64,3072]{2,1,0:T(8,128)(2,1)}, u32[]{:S(2)}, u32[]{:S(2)}) collective-permute-start(bf16[2,64,3072]{2,1,0:T(8,128)(2,1)S(1)} %pad_maximum_fusion), channel_id=1, source_target_pairs={{8,0},{16,8},{24,16},{32,24},{40,32},{48,40},{56,48},{64,56},{72,6... | collective-permute-start | bytes 2359304 | tf_op jit(solution)/shard_map/ppermute | solution.py:31
  50.3 71.9 %collective-permute-start.4 = (bf16[2,48,3072]{2,1,0:T(8,128)(2,1)}, bf16[2,48,3072]{2,1,0:T(8,128)(2,1)S(1)}, u32[]{:S(2)}, u32[]{:S(2)}) collective-permute-start(bf16[2,48,3072]{2,1,0:T(8,128)(2,1)} %slice.72), channel_id=1, source_target_pairs={{0,16},{8,24},{16,32},{24,40},{32,48},{40,56},{48,64},{56,72},{64,... | collective-permute-start | bytes 1769480 | tf_op jit(solution)/shard_map/ppermute | solution.py:31
  72.4 49.8 %collective-permute-start.5 = (bf16[2,48,3072]{2,1,0:T(8,128)(2,1)}, bf16[2,48,3072]{2,1,0:T(8,128)(2,1)}, u32[]{:S(2)}, u32[]{:S(2)}) collective-permute-start(bf16[2,48,3072]{2,1,0:T(8,128)(2,1)} %slice.72), channel_id=1, source_target_pairs={{16,0},{24,8},{32,16},{40,24},{48,32},{56,40},{64,48},{72,56},{80,... | collective-permute-start | bytes 1769480 | tf_op jit(solution)/shard_map/ppermute | solution.py:31
  75.3 4.1 %copy-start.2 = (bf16[2,40,3072]{2,1,0:T(8,128)(2,1)}, bf16[2,40,3072]{2,1,0:T(8,128)(2,1)S(1)}, u32[]{:S(2)}) copy-start(bf16[2,40,3072]{2,1,0:T(8,128)(2,1)S(1)} %collective-permute-done.6) | copy-start | bytes 1474564
  75.3 46.8 %collective-permute-start.7 = (bf16[2,40,3072]{2,1,0:T(8,128)(2,1)}, bf16[2,40,3072]{2,1,0:T(8,128)(2,1)}, u32[]{:S(2)}, u32[]{:S(2)}) collective-permute-start(bf16[2,40,3072]{2,1,0:T(8,128)(2,1)} %slice.73), channel_id=1, source_target_pairs={{32,0},{40,8},{48,16},{56,24},{64,32},{72,40},{80,48},{88,56},{96,... | collective-permute-start | bytes 1474568 | tf_op jit(solution)/shard_map/ppermute | solution.py:31
  160.0 18.8 %copy-start.4 = (f32[24,32]{1,0:T(8,128)}, f32[24,32]{1,0:T(8,128)S(1)}, u32[]{:S(2)}) copy-start(f32[24,32]{1,0:T(8,128)S(1)} %get-tuple-element.34) | copy-start | bytes 9220
  176.0 3.4 %copy-start = (f32[24,32,376]{2,1,0:T(8,128)S(1)}, f32[24,32,376]{2,1,0:T(8,128)}, u32[]{:S(2)}) copy-start(f32[24,32,376]{2,1,0:T(8,128)} %get-tuple-element.35) | copy-start | bytes 3465220
  176.0 4.4 %copy-start.1 = (bf16[1,376,3072]{1,2,0:T(8,128)(2,1)S(1)}, bf16[1,376,3072]{1,2,0:T(8,128)(2,1)}, u32[]{:S(2)}) copy-start(bf16[1,376,3072]{1,2,0:T(8,128)(2,1)} %copy.29) | copy-start | bytes 6930436
  178.8 1.6 copy-start.6
  181.4 6.4 %copy-start.5 = (f32[24,32]{1,0:T(8,128)S(1)}, f32[24,32]{1,0:T(8,128)}, u32[]{:S(2)}) copy-start(f32[24,32]{1,0:T(8,128)} %copy-done.4) | copy-start | bytes 9220
Sparse Core Ops, SparseCore 0:
  9.8 49.6 all-gather.1
where the time goes:
time: 200 us; the launch traced here: 199 us
  waiting for transfers between devices  69.6 us (35%)
  local copies, waits for them, and re-layouts  66.3 us (33%)
  starting transfers between devices  32 us (16%)
  between operations  13.8 us (7%)
  other arithmetic  9.27 us (5%)
  matrix products  7.67 us (4%)
    ppermute x8, waiting for transfers between devices, shifted(): return lax.ppermute(array, axis, pairs)  64.2 us
    ppermute x8, starting transfers between devices, shifted(): return lax.ppermute(array, axis, pairs)  24.6 us
    concatenate x1, local copies, waits for them, and re-layouts, rows_plan(): jnp.concatenate(key_blocks, 1)  24.3 us
    unnamed x20, local copies, waits for them, and re-layouts  13.2 us
    slice x2, local copies, waits for them, and re-layouts, absorb(): value_heads = key_values[1].reshape(key_count, head_count, HD)  13 us
    slice x2, local copies, waits for them, and re-layouts, absorb(): key_heads = key_values[0].reshape(key_count, head_count, HD)  7.73 us
    ppermute x1, starting transfers between devices, extended(): lax.ppermute(lax.slice_in_dim(block, block.shape[dim] - width, None, axis...  5.49 us
    and x4, other arithmetic, rows_plan(): (row_gap <= windows[0, column]) & in_frame[None, :] & present  5.35 us
  transfers between devices with their start and end apart: 11, of which 6 were waited for; matrix products, arithmetic and copies ran while one was open for 24% of the time, Pallas kernels for 0%

commit v1 on v0

v1 whole, which is shorter than its diff:
```python
import functools
import math

import jax
import jax.numpy as jnp
from jax import lax
from jax.experimental import pallas as pl
from jax.experimental.pallas import tpu as pltpu
from jax.sharding import PartitionSpec as P

HD = 128
OCTAVES = 4
Q_ROWS = 64
K_ROWS = 128

neg_large = -1e30
vmem_bytes = 40 * 1024 * 1024


def crossed(array, by, sense):
    length = lax.axis_size("frame")
    signs = [sense if i % 2 == 0 else -sense for i in range(length)]
    return lax.ppermute(array, "frame", [(i, (i + by * s) % length) for i, s in enumerate(signs)])


def dot_nt(left, right):
    return lax.dot_general(
        left, right, (((1,), (1,)), ((), ())), preferred_element_type=jnp.float32
    )


def dot_nn(left, right):
    return lax.dot_general(
        left, right, (((1,), (0,)), ((), ())), preferred_element_type=jnp.float32
    )


def key_start(block, frame_rows):
    return min(max(block * Q_ROWS - (K_ROWS - Q_ROWS) // 2, 0), frame_rows - K_ROWS)


def rows_of(ref, part, at, start=0, count=None):
    whole = ref[:, part, :, at] if part is not None else ref[:, :, at]
    whole = whole.reshape(whole.shape[0] * whole.shape[1], HD)
    return whole if count is None else whole[start : start + count]


def banded(query_block, block, frame_rows, reach, refs, at, lean, scale):
    start = key_start(block, frame_rows)
    gap = jnp.abs(lean + (block * Q_ROWS - start))
    tiles = []
    for ref, limit in zip(refs, reach):
        keys = rows_of(ref, 0, at, start, K_ROWS)
        tiles.append(jnp.where(gap <= limit, dot_nt(query_block, keys) * scale, neg_large))
    return tiles


def folded(tiles, combine):
    while len(tiles) > 1:
        tiles = [
            combine(*tiles[i : i + 2]) if i + 1 < len(tiles) else tiles[i]
            for i in range(0, len(tiles), 2)
        ]
    return tiles[0]


def row_gap():
    return lax.broadcasted_iota(jnp.int32, (Q_ROWS, K_ROWS), 0) - lax.broadcasted_iota(
        jnp.int32, (Q_ROWS, K_ROWS), 1
    )


def weigh(tiles, top):
    weights = [jnp.exp2(tile - top) for tile in tiles]
    total = jnp.sum(folded(weights, jnp.add), axis=1, keepdims=True)
    return jnp.concatenate([w.astype(jnp.bfloat16) for w in weights], 1), total


def near_kernel(frame_rows, columns, scale, reach, queries, own, *refs):
    partner_refs = refs[: len(columns)]
    top_out, sum_out, product_out = refs[len(columns) :]
    lean = row_gap()
    limits = [reach[column] for column in columns]
    blocks = range(frame_rows // Q_ROWS)
    for head in range(queries.shape[2] // HD):
        at = slice(head * HD, (head + 1) * HD)
        all_queries = rows_of(queries, None, at)
        own_keys = rows_of(own, 0, at)
        own_values = rows_of(own, 1, at)
        for block in blocks:
            rows = slice(block * Q_ROWS, (block + 1) * Q_ROWS)
            query_block = all_queries[rows]
            own_scores = dot_nt(query_block, own_keys) * scale
            tiles = [own_scores[:, k : k + K_ROWS] for k in range(0, frame_rows, K_ROWS)]
            tiles += banded(
                query_block, block, frame_rows, limits, partner_refs, at, lean, scale
            )
            top = jnp.max(folded(tiles, jnp.maximum), axis=1, keepdims=True)
            weights, total = weigh(tiles, top)
            start = key_start(block, frame_rows)
            values = [rows_of(ref, 1, at, start, K_ROWS) for ref in partner_refs]
            top_out[head, rows] = jnp.broadcast_to(top, (Q_ROWS, HD))
            sum_out[head, rows] = jnp.broadcast_to(total, (Q_ROWS, HD))
            product_out[head, rows] = dot_nn(weights, jnp.concatenate([own_values] + values, 0))


def far_kernel(frame_rows, columns, scale, reach, queries, top_in, sum_in, product_in, *refs):
    partner_refs = refs[: len(columns)]
    out = refs[len(columns)]
    lean = row_gap()
    limits = [reach[column] for column in columns]
    parts = Q_ROWS // out.shape[1]
    blocks = range(frame_rows // Q_ROWS)
    span = [slice(block * Q_ROWS, (block + 1) * Q_ROWS) for block in blocks]
    for head in range(queries.shape[2] // HD):
        at = slice(head * HD, (head + 1) * HD)
        all_queries = rows_of(queries, None, at)
        tiles = [
            banded(all_queries[span[b]], b, frame_rows, limits, partner_refs, at, lean, scale)
            for b in blocks
        ]
        tops = [
            jnp.maximum(
                top_in[head, span[b]],
                jnp.max(folded(tiles[b], jnp.maximum), axis=1, keepdims=True),
            )
            for b in blocks
        ]
        weighed = [weigh(tiles[b], tops[b]) for b in blocks]
        products = [
            dot_nn(
                weighed[b][0],
                jnp.concatenate(
                    [
                        rows_of(ref, 1, at, key_start(b, frame_rows), K_ROWS)
                        for ref in partner_refs
                    ],
                    0,
                ),
            )
            for b in blocks
        ]
        for b in blocks:
            shrink = jnp.exp2(top_in[head, span[b]] - tops[b])
            total = sum_in[head, span[b]] * shrink + weighed[b][1]
            product = product_in[head, span[b]] * shrink + products[b]
            out[b * parts : (b + 1) * parts, :, at] = (
                (product / total).astype(jnp.bfloat16).reshape(parts, out.shape[1], HD)
            )


def near_call(reach, queries, own, partners, columns, scale):
    space, rows, feat = queries.shape
    state = jax.ShapeDtypeStruct((feat // HD, space * rows, HD), jnp.float32)
    return pl.pallas_call(
        functools.partial(near_kernel, space * rows, columns, scale),
        in_specs=[pl.BlockSpec(memory_space=pltpu.SMEM)]
        + [pl.BlockSpec(memory_space=pltpu.VMEM)] * (2 + len(columns)),
        out_specs=[pl.BlockSpec(memory_space=pltpu.VMEM)] * 3,
        out_shape=[state] * 3,
        compiler_params=pltpu.CompilerParams(vmem_limit_bytes=vmem_bytes),
        cost_estimate=pl.CostEstimate(
            flops=1_000_000_000, bytes_accessed=6_000_000, transcendentals=1_000_000
        ),
        name="own_and_near",
    )(reach, queries, own, *partners)


def far_call(reach, queries, state, partners, columns, scale):
    space, rows, feat = queries.shape
    return pl.pallas_call(
        functools.partial(far_kernel, space * rows, columns, scale),
        in_specs=[pl.BlockSpec(memory_space=pltpu.SMEM)]
        + [pl.BlockSpec(memory_space=pltpu.VMEM)] * (4 + len(columns)),
        out_specs=pl.BlockSpec(memory_space=pltpu.VMEM),
        out_shape=jax.ShapeDtypeStruct((space, rows, feat), jnp.bfloat16),
        compiler_params=pltpu.CompilerParams(vmem_limit_bytes=vmem_bytes),
        cost_estimate=pl.CostEstimate(
            flops=2_000_000_000, bytes_accessed=4_000_000, transcendentals=500_000
        ),
        name="far_and_merge",
    )(reach, queries, *state, *partners)


def heads_plan(queries, keys, values, windows, scale):
    rows, feat = queries.shape[1:]
    space = lax.axis_size("space")
    frame_pos = lax.axis_index("frame")
    frame_count = lax.axis_size("frame")
    wide = feat // space

    distance = 2 ** jnp.arange(OCTAVES, dtype=jnp.int32)
    below = jnp.where(frame_pos - distance >= 0, windows[0, 0::2], -1)
    above = jnp.where(frame_pos + distance < frame_count, windows[0, 1::2], -1)
    upper = ((frame_pos & 1) == 0) == (distance == 1)
    reach = jnp.concatenate([jnp.where(upper, above, below), jnp.where(upper, below, above)])

    pair = jnp.stack([keys[0], values[0]]).reshape(2, rows, space, wide)
    own = lax.all_to_all(jnp.transpose(pair, (2, 0, 1, 3)), "space", 0, 0, tiled=True)

    split = jnp.transpose(queries[0].reshape(rows, space, wide), (1, 0, 2))
    first_eight = crossed(own, 8, 1)
    first_two = crossed(own, 2, 1)
    second_two = crossed(own, 2, -1)
    first_one = crossed(own, 1, 1)
    split = lax.all_to_all(split, "space", 0, 0, tiled=True)
    first_two, second_two, split = lax.optimization_barrier((first_two, second_two, split))
    first_four = crossed(first_two, 2, 1)
    second_four = crossed(second_two, 2, -1)
    own_late, _ = lax.optimization_barrier((own, first_two))
    second_one = crossed(own_late, 1, -1)
    second_eight = crossed(first_eight, 16, -1)

    near = [first_one, second_one, first_two, second_two]
    state = near_call(reach, split, own, near, [0, 4, 1, 5], scale)
    far = [first_four, second_four, first_eight, second_eight]
    result = far_call(
        reach, split, state, far, [2, 6, 3, 7], scale
    )
    result = lax.all_to_all(result, "space", 0, 0, tiled=True)
    return jnp.transpose(result, (1, 0, 2)).reshape(1, rows, feat)


def shards(queries, keys, values, windows):
    scale = math.log2(math.e) / math.sqrt(HD)
    return heads_plan(queries, keys, values, windows, scale)


def solution(mesh):
    return jax.shard_map(
        shards,
        mesh=mesh,
        in_specs=(
            P("frame", "space", None),
            P("frame", "space", None),
            P("frame", "space", None),
            P("frame", None),
        ),
        out_specs=P("frame", "space", None),
        check_vma=False,
    )
```

time: 200 us -> 98.2 us (0.49)
  the two profiles are of different devices: /device:TPU:200 before, /device:TPU:1 now
where the time goes in v1:
time: 98.2 us; the launch traced here: 97.6 us
  blocking collectives  38.9 us (40%)
  starting transfers between devices  37.2 us (38%)
  waiting for transfers between devices  11 us (11%)
  Pallas kernels  7.25 us (7%)
  local copies, waits for them, and re-layouts  1.81 us (2%)
  other arithmetic  1.15 us (1%)
    ppermute x8, starting transfers between devices, crossed(): lax.ppermute(array, 'frame', [(i, (i + by * s) % length) for i, s in enum...  33.8 us
    all_to_all x1, blocking collectives, heads_plan(): lax.all_to_all(jnp.transpose(pair, (2, 0, 1, 3)), 'space', 0, 0, tiled=True)  24.3 us
    all_to_all x1, blocking collectives, heads_plan(): result = lax.all_to_all(result, 'space', 0, 0, tiled=True)  14.6 us
    ppermute x8, waiting for transfers between devices, crossed(): lax.ppermute(array, 'frame', [(i, (i + by * s) % length) for i, s in enum...  11 us
    pallas_call x1, Pallas kernels, near_call(): pl.pallas_call(functools.partial(near_kernel, space * rows, columns, scal...  4.8 us
    all_to_all x1, starting transfers between devices, heads_plan(): split = lax.all_to_all(split, 'space', 0, 0, tiled=True)  3.39 us
    pallas_call x1, Pallas kernels, far_call(): pl.pallas_call(functools.partial(far_kernel, space * rows, columns, scale...  2.45 us
  transfers between devices with their start and end apart: 9, of which 2 were waited for; matrix products, arithmetic and copies ran while one was open for 1% of the time, Pallas kernels for 5%

profile of v1, /device:TPU:1, one launch (start us, length us, event | category | flops | bytes accessed | tf_op | source)
XLA Modules:
  0.0 97.6 jit_solution(10884340688980427581)
XLA Ops:
  0.0 1.1 %pad_maximum_fusion = bf16[2,32,3072]{2,1,0:T(8,128)(2,1)S(1)} fusion(bf16[1,32,3072]{2,1,0:T(8,128)(2,1)} %param.6, bf16[1,32,3072]{2,1,0:T(8,128)(2,1)} %param.5), kind=kLoop, calls=%fused_computation.1 | loop fusion | flops 196608 | bytes 786432 | tf_op jit(solution)/shard_map/stack | solution.py:198
  1.1 0.0 copy-start
  1.1 24.3 %all_to_all.15.own = bf16[8,2,32,384]{3,2,1,0:T(8,128)(2,1)S(1)} all-to-all(bf16[8,2,32,384]{3,2,1,0:T(8,128)(2,1)S(1)} %bitcast.26), channel_id=1, replica_groups=mesh['frame'=64,'space'=8] {'space'}, dimensions={0} | all-to-all | bytes 786432 | tf_op jit(solution)/shard_map/all_to_all | solution.py:199
  25.4 7.3 %collective-permute-start = (bf16[8,2,32,384]{3,2,1,0:T(8,128)(2,1)S(1)}, bf16[8,2,32,384]{3,2,1,0:T(8,128)(2,1)S(1)}, u32[]{:S(2)}, u32[]{:S(2)}) collective-permute-start(bf16[8,2,32,384]{3,2,1,0:T(8,128)(2,1)S(1)} %all_to_all.15.own), channel_id=1, source_target_pairs={{0,16},{8,504},{16,32},{24,8},{32,48},{40,24},{48,64},{56,40},{64,... | collective-permute-start | bytes 1179656 | tf_op jit(solution)/shard_map/ppermute | solution.py:23
  32.7 1.9 %collective-permute-start.1 = (bf16[8,2,32,384]{3,2,1,0:T(8,128)(2,1)S(1)}, bf16[8,2,32,384]{3,2,1,0:T(8,128)(2,1)S(1)}, u32[]{:S(2)}, u32[]{:S(2)}) collective-permute-start(bf16[8,2,32,384]{3,2,1,0:T(8,128)(2,1)S(1)} %all_to_all.15.own), channel_id=1, source_target_pairs={{0,496},{8,24},{16,0},{24,40},{32,16},{40,56},{48,32},{56,72},{64,... | collective-permute-start | bytes 1179656 | tf_op jit(solution)/shard_map/ppermute | solution.py:23
  34.7 0.0 copy-done
  34.7 0.7 copy.13
  35.4 3.4 %all-to-all-start.1 = ((bf16[8,32,384]{2,1,0:T(8,128)(2,1)}), bf16[8,32,384]{2,1,0:T(8,128)(2,1)S(1)}, u32[]{:S(2)}, u32[]{:S(2)}) async-start(bf16[8,32,384]{2,1,0:T(8,128)(2,1)} %bitcast.25), calls=%async_computation.1 | async-start | bytes 393216 | tf_op jit(solution)/shard_map/all_to_all | solution.py:206
  38.8 0.0 copy-start.1
  38.8 5.7 %collective-permute-start.6 = (bf16[8,2,32,384]{3,2,1,0:T(8,128)(2,1)S(1)}, bf16[8,2,32,384]{3,2,1,0:T(8,128)(2,1)S(1)}, u32[]{:S(2)}, u32[]{:S(2)}) collective-permute-start(bf16[8,2,32,384]{3,2,1,0:T(8,128)(2,1)S(1)} %all_to_all.15.own), channel_id=1, source_target_pairs={{0,64},{8,456},{16,80},{24,472},{32,96},{40,488},{48,112},{56,504}... | collective-permute-start | bytes 1179656 | tf_op jit(solution)/shard_map/ppermute | solution.py:23
  44.5 3.9 %collective-permute-start.2 = (bf16[8,2,32,384]{3,2,1,0:T(8,128)(2,1)S(1)}, bf16[8,2,32,384]{3,2,1,0:T(8,128)(2,1)S(1)}, u32[]{:S(2)}, u32[]{:S(2)}) collective-permute-start(bf16[8,2,32,384]{3,2,1,0:T(8,128)(2,1)S(1)} %all_to_all.15.own), channel_id=1, source_target_pairs={{0,8},{8,0},{16,24},{24,16},{32,40},{40,32},{48,56},{56,48},{64,72... | collective-permute-start | bytes 1179656 | tf_op jit(solution)/shard_map/ppermute | solution.py:23
  48.4 0.0 all-to-all-done.1.queries
  48.4 0.0 collective-permute-done.refs_2_
  48.5 0.0 collective-permute-done.1.refs_3_
  48.5 1.9 %collective-permute-start.3 = (bf16[8,2,32,384]{3,2,1,0:T(8,128)(2,1)S(1)}, bf16[8,2,32,384]{3,2,1,0:T(8,128)(2,1)S(1)}, u32[]{:S(2)}, u32[]{:S(2)}) collective-permute-start(bf16[8,2,32,384]{3,2,1,0:T(8,128)(2,1)S(1)} %all_to_all.15.own), channel_id=1, source_target_pairs={{0,504},{8,16},{16,8},{24,32},{32,24},{40,48},{48,40},{56,64},{64,... | collective-permute-start | bytes 1179656 | tf_op jit(solution)/shard_map/ppermute | solution.py:23
  50.4 0.0 copy-done.1
  50.4 0.1 slice.6
  50.5 0.1 slice.7
  50.6 9.0 %collective-permute-start.4 = (bf16[8,2,32,384]{3,2,1,0:T(8,128)(2,1)S(1)}, bf16[8,2,32,384]{3,2,1,0:T(8,128)(2,1)S(1)}, u32[]{:S(2)}, u32[]{:S(2)}) collective-permute-start(bf16[8,2,32,384]{3,2,1,0:T(8,128)(2,1)S(1)} %collective-permute-done.refs_2_), channel_id=1, source_target_pairs={{0,16},{8,504},{16,32},{24,8},{32,48},{40,24},{48,64},{56,40},{64,... | collective-permute-start | bytes 1179656 | tf_op jit(solution)/shard_map/ppermute | solution.py:23
  59.6 1.9 %collective-permute-start.5 = (bf16[8,2,32,384]{3,2,1,0:T(8,128)(2,1)S(1)}, bf16[8,2,32,384]{3,2,1,0:T(8,128)(2,1)S(1)}, u32[]{:S(2)}, u32[]{:S(2)}) collective-permute-start(bf16[8,2,32,384]{3,2,1,0:T(8,128)(2,1)S(1)} %collective-permute-done.1.refs_3_), channel_id=1, source_target_pairs={{0,496},{8,24},{16,0},{24,40},{32,16},{40,56},{48,32},{56,72},{64,... | collective-permute-start | bytes 1179656 | tf_op jit(solution)/shard_map/ppermute | solution.py:23
  61.5 0.0 collective-permute-done.6.refs_2_
  61.5 2.2 %collective-permute-start.7 = (bf16[8,2,32,384]{3,2,1,0:T(8,128)(2,1)S(1)}, bf16[8,2,32,384]{3,2,1,0:T(8,128)(2,1)S(1)}, u32[]{:S(2)}, u32[]{:S(2)}) collective-permute-start(bf16[8,2,32,384]{3,2,1,0:T(8,128)(2,1)S(1)} %collective-permute-done.6.refs_2_), channel_id=1, source_target_pairs={{0,384},{8,136},{16,400},{24,152},{32,416},{40,168},{48,432},{56,1... | collective-permute-start | bytes 1179656 | tf_op jit(solution)/shard_map/ppermute | solution.py:23
  63.8 0.1 pad_add_fusion.reach
  63.8 0.0 collective-permute-done.2.refs_0_
  63.8 7.6 %collective-permute-done.3.refs_1_ = bf16[8,2,32,384]{3,2,1,0:T(8,128)(2,1)S(1)} collective-permute-done((bf16[8,2,32,384]{3,2,1,0:T(8,128)(2,1)S(1)}, bf16[8,2,32,384]{3,2,1,0:T(8,128)(2,1)S(1)}, u32[]{:S(2)}, u32[]{:S(2)}) %collective-permute-start.3) | collective-permute-done | bytes 393248 | tf_op jit(solution)/shard_map/ppermute | solution.py:23
  71.5 4.8 %own_and_near.1 = (f32[3,256,128]{2,1,0:T(8,128)S(1)}, f32[3,256,128]{2,1,0:T(8,128)S(1)}, f32[3,256,128]{2,1,0:T(8,128)S(1)}) custom-call(s32[8]{0:T(128)S(1)} %pad_add_fusion.reach, bf16[8,32,384]{2,1,0:T(8,128)(2,1)S(1)} %all-to-all-done.1.queries, bf16[8,2,32,384]{3,2,1,0:T(8,128)(2,1)S(1)} %all_to_all.15.own, ...), custom_call_target="tpu_custom_call" | custom-call | flops 1000000000 | bytes 6000000 | tf_op jit(solution)/shard_map/own_and_near/pallas_call | solution.py:155
  76.3 0.0 collective-permute-done.4.refs_0_
  76.3 0.0 collective-permute-done.5.refs_1_
  76.3 3.4 %collective-permute-done.7.refs_3_ = bf16[8,2,32,384]{3,2,1,0:T(8,128)(2,1)S(1)} collective-permute-done((bf16[8,2,32,384]{3,2,1,0:T(8,128)(2,1)S(1)}, bf16[8,2,32,384]{3,2,1,0:T(8,128)(2,1)S(1)}, u32[]{:S(2)}, u32[]{:S(2)}) %collective-permute-start.7) | collective-permute-done | bytes 393248 | tf_op jit(solution)/shard_map/ppermute | solution.py:23
  79.7 2.4 %far_and_merge.1 = bf16[8,32,384]{2,1,0:T(8,128)(2,1)S(1)} custom-call(s32[8]{0:T(128)S(1)} %pad_add_fusion.reach, bf16[8,32,384]{2,1,0:T(8,128)(2,1)S(1)} %all-to-all-done.1.queries, f32[3,256,128]{2,1,0:T(8,128)S(1)} %get-tuple-element.16.top_in, f32[3,256,128]{2,1,0:T(8,128)S(1)} %get-tuple-element.17.sum_in, ...), custom_call_target="tpu_custom_call" | custom-call | flops 2000000000 | bytes 4000000 | tf_op jit(solution)/shard_map/far_and_merge/pallas_call | solution.py:171
  82.1 14.6 %all_to_all.16 = bf16[8,32,384]{2,1,0:T(8,128)(2,1)S(1)} all-to-all(bf16[8,32,384]{2,1,0:T(8,128)(2,1)S(1)} %far_and_merge.1), channel_id=1, replica_groups=mesh['frame'=64,'space'=8] {'space'}, dimensions={0} | all-to-all | bytes 393216 | tf_op jit(solution)/shard_map/all_to_all | solution.py:220
  96.8 0.1 copy.7
  96.8 0.8 reshape.7
  (3 shorter events, 0.1 us)
Async XLA Ops:
  1.1 33.5 %copy-start = (bf16[1,32,3072]{2,1,0:T(8,128)(2,1)S(1)}, bf16[1,32,3072]{2,1,0:T(8,128)(2,1)}, u32[]{:S(2)}) copy-start(bf16[1,32,3072]{2,1,0:T(8,128)(2,1)} %param.4) | copy-start | bytes 589828
  25.4 23.0 %collective-permute-start = (bf16[8,2,32,384]{3,2,1,0:T(8,128)(2,1)S(1)}, bf16[8,2,32,384]{3,2,1,0:T(8,128)(2,1)S(1)}, u32[]{:S(2)}, u32[]{:S(2)}) collective-permute-start(bf16[8,2,32,384]{3,2,1,0:T(8,128)(2,1)S(1)} %all_to_all.15.own), channel_id=1, source_target_pairs={{0,16},{8,504},{16,32},{24,8},{32,48},{40,24},{48,64},{56,40},{64,... | collective-permute-start | bytes 1179656 | tf_op jit(solution)/shard_map/ppermute | solution.py:23
  32.7 15.7 %collective-permute-start.1 = (bf16[8,2,32,384]{3,2,1,0:T(8,128)(2,1)S(1)}, bf16[8,2,32,384]{3,2,1,0:T(8,128)(2,1)S(1)}, u32[]{:S(2)}, u32[]{:S(2)}) collective-permute-start(bf16[8,2,32,384]{3,2,1,0:T(8,128)(2,1)S(1)} %all_to_all.15.own), channel_id=1, source_target_pairs={{0,496},{8,24},{16,0},{24,40},{32,16},{40,56},{48,32},{56,72},{64,... | collective-permute-start | bytes 1179656 | tf_op jit(solution)/shard_map/ppermute | solution.py:23
  35.4 13.0 %all-to-all-start.1 = ((bf16[8,32,384]{2,1,0:T(8,128)(2,1)}), bf16[8,32,384]{2,1,0:T(8,128)(2,1)S(1)}, u32[]{:S(2)}, u32[]{:S(2)}) async-start(bf16[8,32,384]{2,1,0:T(8,128)(2,1)} %bitcast.25), calls=%async_computation.1 | async-start | bytes 393216 | tf_op jit(solution)/shard_map/all_to_all | solution.py:206
  38.8 11.6 %copy-start.1 = (s32[1,8]{1,0:T(1,128)S(1)}, s32[1,8]{1,0:T(1,128)}, u32[]{:S(2)}) copy-start(s32[1,8]{1,0:T(1,128)} %param.7) | copy-start | bytes 100
  38.8 22.7 %collective-permute-start.6 = (bf16[8,2,32,384]{3,2,1,0:T(8,128)(2,1)S(1)}, bf16[8,2,32,384]{3,2,1,0:T(8,128)(2,1)S(1)}, u32[]{:S(2)}, u32[]{:S(2)}) collective-permute-start(bf16[8,2,32,384]{3,2,1,0:T(8,128)(2,1)S(1)} %all_to_all.15.own), channel_id=1, source_target_pairs={{0,64},{8,456},{16,80},{24,472},{32,96},{40,488},{48,112},{56,504}... | collective-permute-start | bytes 1179656 | tf_op jit(solution)/shard_map/ppermute | solution.py:23
  44.5 19.3 %collective-permute-start.2 = (bf16[8,2,32,384]{3,2,1,0:T(8,128)(2,1)S(1)}, bf16[8,2,32,384]{3,2,1,0:T(8,128)(2,1)S(1)}, u32[]{:S(2)}, u32[]{:S(2)}) collective-permute-start(bf16[8,2,32,384]{3,2,1,0:T(8,128)(2,1)S(1)} %all_to_all.15.own), channel_id=1, source_target_pairs={{0,8},{8,0},{16,24},{24,16},{32,40},{40,32},{48,56},{56,48},{64,72... | collective-permute-start | bytes 1179656 | tf_op jit(solution)/shard_map/ppermute | solution.py:23
  48.5 23.0 %collective-permute-start.3 = (bf16[8,2,32,384]{3,2,1,0:T(8,128)(2,1)S(1)}, bf16[8,2,32,384]{3,2,1,0:T(8,128)(2,1)S(1)}, u32[]{:S(2)}, u32[]{:S(2)}) collective-permute-start(bf16[8,2,32,384]{3,2,1,0:T(8,128)(2,1)S(1)} %all_to_all.15.own), channel_id=1, source_target_pairs={{0,504},{8,16},{16,8},{24,32},{32,24},{40,48},{48,40},{56,64},{64,... | collective-permute-start | bytes 1179656 | tf_op jit(solution)/shard_map/ppermute | solution.py:23
  50.6 25.7 %collective-permute-start.4 = (bf16[8,2,32,384]{3,2,1,0:T(8,128)(2,1)S(1)}, bf16[8,2,32,384]{3,2,1,0:T(8,128)(2,1)S(1)}, u32[]{:S(2)}, u32[]{:S(2)}) collective-permute-start(bf16[8,2,32,384]{3,2,1,0:T(8,128)(2,1)S(1)} %collective-permute-done.refs_2_), channel_id=1, source_target_pairs={{0,16},{8,504},{16,32},{24,8},{32,48},{40,24},{48,64},{56,40},{64,... | collective-permute-start | bytes 1179656 | tf_op jit(solution)/shard_map/ppermute | solution.py:23
  59.6 16.7 %collective-permute-start.5 = (bf16[8,2,32,384]{3,2,1,0:T(8,128)(2,1)S(1)}, bf16[8,2,32,384]{3,2,1,0:T(8,128)(2,1)S(1)}, u32[]{:S(2)}, u32[]{:S(2)}) collective-permute-start(bf16[8,2,32,384]{3,2,1,0:T(8,128)(2,1)S(1)} %collective-permute-done.1.refs_3_), channel_id=1, source_target_pairs={{0,496},{8,24},{16,0},{24,40},{32,16},{40,56},{48,32},{56,72},{64,... | collective-permute-start | bytes 1179656 | tf_op jit(solution)/shard_map/ppermute | solution.py:23
  61.5 18.1 %collective-permute-start.7 = (bf16[8,2,32,384]{3,2,1,0:T(8,128)(2,1)S(1)}, bf16[8,2,32,384]{3,2,1,0:T(8,128)(2,1)S(1)}, u32[]{:S(2)}, u32[]{:S(2)}) collective-permute-start(bf16[8,2,32,384]{3,2,1,0:T(8,128)(2,1)S(1)} %collective-permute-done.6.refs_2_), channel_id=1, source_target_pairs={{0,384},{8,136},{16,400},{24,152},{32,416},{40,168},{48,432},{56,1... | collective-permute-start | bytes 1179656 | tf_op jit(solution)/shard_map/ppermute | solution.py:23

commit v2 on v1

--- a/solution.py
+++ b/solution.py
@@ -200,23 +200,22 @@
 
     split = jnp.transpose(queries[0].reshape(rows, space, wide), (1, 0, 2))
     first_eight = crossed(own, 8, 1)
+    first_one = crossed(own, 1, 1)
     first_two = crossed(own, 2, 1)
-    second_two = crossed(own, 2, -1)
-    first_one = crossed(own, 1, 1)
+    second_one = crossed(first_one, 2, 1)
+    second_two = crossed(second_one, 1, 1)
+    first_four = crossed(first_two, 2, 1)
+    three = crossed(second_one, 2, 1)
+    second_four = crossed(three, 1, 1)
+    split, _ = lax.optimization_barrier((split, first_two))
     split = lax.all_to_all(split, "space", 0, 0, tiled=True)
-    first_two, second_two, split = lax.optimization_barrier((first_two, second_two, split))
-    first_four = crossed(first_two, 2, 1)
-    second_four = crossed(second_two, 2, -1)
-    own_late, _ = lax.optimization_barrier((own, first_two))
-    second_one = crossed(own_late, 1, -1)
+    first_eight, split = lax.optimization_barrier((first_eight, split))
     second_eight = crossed(first_eight, 16, -1)
 
-    near = [first_one, second_one, first_two, second_two]
-    state = near_call(reach, split, own, near, [0, 4, 1, 5], scale)
-    far = [first_four, second_four, first_eight, second_eight]
-    result = far_call(
-        reach, split, state, far, [2, 6, 3, 7], scale
-    )
+    near = [first_one, second_one, first_two, first_four]
+    state = near_call(reach, split, own, near, [0, 4, 1, 2], scale)
+    far = [second_two, second_four, first_eight, second_eight]
+    result = far_call(reach, split, state, far, [5, 6, 3, 7], scale)
     result = lax.all_to_all(result, "space", 0, 0, tiled=True)
     return jnp.transpose(result, (1, 0, 2)).reshape(1, rows, feat)
 

time: 98.2 us -> 107 us (1.090)
  waiting for transfers between devices: 11 us -> 15.7 us
  starting transfers between devices: 37.2 us -> 39.9 us
  blocking collectives: 38.9 us -> 40.4 us
    ppermute x8 -> x9, waiting for transfers between devices: 11 us -> 14.5 us  [crossed(): lax.ppermute(array, 'frame', [(i, (i + by * s) % length) for i, s in enum...]
    ppermute x8 -> x9, starting transfers between devices: 33.8 us -> 36.5 us  [crossed(): lax.ppermute(array, 'frame', [(i, (i + by * s) % length) for i, s in enum...]
    all_to_all x1, blocking collectives: 14.6 us -> 16.1 us  [heads_plan(): result = lax.all_to_all(result, 'space', 0, 0, tiled=True)]
    all_to_all x1, waiting for transfers between devices: 0.01 us -> 1.18 us  [heads_plan(): split = lax.all_to_all(split, 'space', 0, 0, tiled=True)]
  transfers between devices with their start and end apart: 9 -> 10, of which waited for: 2 -> 3; matrix products, arithmetic and copies ran while one was open for 1% -> 1% of each run, Pallas kernels for 5% -> 5%
where the time goes in v2:
time: 107 us; the launch traced here: 106 us
  blocking collectives  40.4 us (38%)
  starting transfers between devices  39.9 us (37%)
  waiting for transfers between devices  15.7 us (15%)
  Pallas kernels  7.25 us (7%)
  local copies, waits for them, and re-layouts  1.81 us (2%)
  other arithmetic  1.15 us (1%)
    ppermute x9, starting transfers between devices, crossed(): lax.ppermute(array, 'frame', [(i, (i + by * s) % length) for i, s in enum...  36.5 us
    all_to_all x1, blocking collectives, heads_plan(): lax.all_to_all(jnp.transpose(pair, (2, 0, 1, 3)), 'space', 0, 0, tiled=True)  24.3 us
    all_to_all x1, blocking collectives, heads_plan(): result = lax.all_to_all(result, 'space', 0, 0, tiled=True)  16.1 us
    ppermute x9, waiting for transfers between devices, crossed(): lax.ppermute(array, 'frame', [(i, (i + by * s) % length) for i, s in enum...  14.5 us
    pallas_call x1, Pallas kernels, near_call(): pl.pallas_call(functools.partial(near_kernel, space * rows, columns, scal...  4.8 us
    all_to_all x1, starting transfers between devices, heads_plan(): split = lax.all_to_all(split, 'space', 0, 0, tiled=True)  3.39 us
    pallas_call x1, Pallas kernels, far_call(): pl.pallas_call(functools.partial(far_kernel, space * rows, columns, scale...  2.45 us
  transfers between devices with their start and end apart: 10, of which 3 were waited for; matrix products, arithmetic and copies ran while one was open for 1% of the time, Pallas kernels for 5%

profile of v2, /device:TPU:1, one launch (start us, length us, event | category | flops | bytes accessed | tf_op | source)
XLA Modules:
  0.0 106.4 jit_solution(17411252910387475699)
XLA Ops:
  0.0 1.1 pad_maximum_fusion
  1.1 0.0 copy-start
  1.1 24.3 %all_to_all.15.own = bf16[8,2,32,384]{3,2,1,0:T(8,128)(2,1)S(1)} all-to-all(bf16[8,2,32,384]{3,2,1,0:T(8,128)(2,1)S(1)} %bitcast.26), channel_id=1, replica_groups=mesh['frame'=64,'space'=8] {'space'}, dimensions={0} | all-to-all | bytes 786432 | tf_op jit(solution)/shard_map/all_to_all | solution.py:199
  25.4 4.0 %collective-permute-start.2 = (bf16[8,2,32,384]{3,2,1,0:T(8,128)(2,1)S(1)}, bf16[8,2,32,384]{3,2,1,0:T(8,128)(2,1)S(1)}, u32[]{:S(2)}, u32[]{:S(2)}) collective-permute-start(bf16[8,2,32,384]{3,2,1,0:T(8,128)(2,1)S(1)} %all_to_all.15.own), channel_id=1, source_target_pairs={{0,8},{8,0},{16,24},{24,16},{32,40},{40,32},{48,56},{56,48},{64,72... | collective-permute-start | bytes 1179656 | tf_op jit(solution)/shard_map/ppermute | solution.py:23
  29.5 1.3 %collective-permute-done.2.refs_0_ = bf16[8,2,32,384]{3,2,1,0:T(8,128)(2,1)S(1)} collective-permute-done((bf16[8,2,32,384]{3,2,1,0:T(8,128)(2,1)S(1)}, bf16[8,2,32,384]{3,2,1,0:T(8,128)(2,1)S(1)}, u32[]{:S(2)}, u32[]{:S(2)}) %collective-permute-start.2) | collective-permute-done | bytes 393248 | tf_op jit(solution)/shard_map/ppermute | solution.py:23
  30.8 7.3 %collective-permute-start.3 = (bf16[8,2,32,384]{3,2,1,0:T(8,128)(2,1)S(1)}, bf16[8,2,32,384]{3,2,1,0:T(8,128)(2,1)S(1)}, u32[]{:S(2)}, u32[]{:S(2)}) collective-permute-start(bf16[8,2,32,384]{3,2,1,0:T(8,128)(2,1)S(1)} %collective-permute-done.2.refs_0_), channel_id=1, source_target_pairs={{0,16},{8,504},{16,32},{24,8},{32,48},{40,24},{48,64},{56,40},{64,... | collective-permute-start | bytes 1179656 | tf_op jit(solution)/shard_map/ppermute | solution.py:23
  38.1 3.0 %collective-permute-start.1 = (bf16[8,2,32,384]{3,2,1,0:T(8,128)(2,1)S(1)}, bf16[8,2,32,384]{3,2,1,0:T(8,128)(2,1)S(1)}, u32[]{:S(2)}, u32[]{:S(2)}) collective-permute-start(bf16[8,2,32,384]{3,2,1,0:T(8,128)(2,1)S(1)} %all_to_all.15.own), channel_id=1, source_target_pairs={{0,16},{8,504},{16,32},{24,8},{32,48},{40,24},{48,64},{56,40},{64,... | collective-permute-start | bytes 1179656 | tf_op jit(solution)/shard_map/ppermute | solution.py:23
  41.1 3.5 %collective-permute-start = (bf16[8,2,32,384]{3,2,1,0:T(8,128)(2,1)S(1)}, bf16[8,2,32,384]{3,2,1,0:T(8,128)(2,1)S(1)}, u32[]{:S(2)}, u32[]{:S(2)}) collective-permute-start(bf16[8,2,32,384]{3,2,1,0:T(8,128)(2,1)S(1)} %all_to_all.15.own), channel_id=1, source_target_pairs={{0,64},{8,456},{16,80},{24,472},{32,96},{40,488},{48,112},{56,504}... | collective-permute-start | bytes 1179656 | tf_op jit(solution)/shard_map/ppermute | solution.py:23
  44.6 0.0 collective-permute-done.3.refs_1_
  44.6 5.3 %collective-permute-start.6 = (bf16[8,2,32,384]{3,2,1,0:T(8,128)(2,1)S(1)}, bf16[8,2,32,384]{3,2,1,0:T(8,128)(2,1)S(1)}, u32[]{:S(2)}, u32[]{:S(2)}) collective-permute-start(bf16[8,2,32,384]{3,2,1,0:T(8,128)(2,1)S(1)} %collective-permute-done.3.refs_1_), channel_id=1, source_target_pairs={{0,16},{8,504},{16,32},{24,8},{32,48},{40,24},{48,64},{56,40},{64,... | collective-permute-start | bytes 1179656 | tf_op jit(solution)/shard_map/ppermute | solution.py:23
  49.9 0.0 copy-done
  50.0 0.7 copy.13
  50.7 13.2 %collective-permute-done.1.refs_2_ = bf16[8,2,32,384]{3,2,1,0:T(8,128)(2,1)S(1)} collective-permute-done((bf16[8,2,32,384]{3,2,1,0:T(8,128)(2,1)S(1)}, bf16[8,2,32,384]{3,2,1,0:T(8,128)(2,1)S(1)}, u32[]{:S(2)}, u32[]{:S(2)}) %collective-permute-start.1) | collective-permute-done | bytes 393248 | tf_op jit(solution)/shard_map/ppermute | solution.py:23
  63.9 3.4 %all-to-all-start.1 = ((bf16[8,32,384]{2,1,0:T(8,128)(2,1)}), bf16[8,32,384]{2,1,0:T(8,128)(2,1)S(1)}, u32[]{:S(2)}, u32[]{:S(2)}) async-start(bf16[8,32,384]{2,1,0:T(8,128)(2,1)} %bitcast.25), calls=%async_computation.1 | async-start | bytes 393216 | tf_op jit(solution)/shard_map/all_to_all | solution.py:211
  67.3 0.0 copy-start.1
  67.3 7.1 %collective-permute-start.4 = (bf16[8,2,32,384]{3,2,1,0:T(8,128)(2,1)S(1)}, bf16[8,2,32,384]{3,2,1,0:T(8,128)(2,1)S(1)}, u32[]{:S(2)}, u32[]{:S(2)}) collective-permute-start(bf16[8,2,32,384]{3,2,1,0:T(8,128)(2,1)S(1)} %collective-permute-done.1.refs_2_), channel_id=1, source_target_pairs={{0,16},{8,504},{16,32},{24,8},{32,48},{40,24},{48,64},{56,40},{64,... | collective-permute-start | bytes 1179656 | tf_op jit(solution)/shard_map/ppermute | solution.py:23
  74.4 0.0 copy-done.1
  74.4 0.1 slice.6
  74.5 0.1 slice.7
  74.6 0.0 collective-permute-done.refs_2_
  74.6 1.2 %all-to-all-done.1.queries = bf16[8,32,384]{2,1,0:T(8,128)(2,1)S(1)} async-done(((bf16[8,32,384]{2,1,0:T(8,128)(2,1)}), bf16[8,32,384]{2,1,0:T(8,128)(2,1)S(1)}, u32[]{:S(2)}, u32[]{:S(2)}) %all-to-all-start.1) | async-done | bytes 196640 | tf_op jit(solution)/shard_map/all_to_all | solution.py:211
  75.8 1.9 %collective-permute-start.8 = (bf16[8,2,32,384]{3,2,1,0:T(8,128)(2,1)S(1)}, bf16[8,2,32,384]{3,2,1,0:T(8,128)(2,1)S(1)}, u32[]{:S(2)}, u32[]{:S(2)}) collective-permute-start(bf16[8,2,32,384]{3,2,1,0:T(8,128)(2,1)S(1)} %collective-permute-done.refs_2_), channel_id=1, source_target_pairs={{0,384},{8,136},{16,400},{24,152},{32,416},{40,168},{48,432},{56,1... | collective-permute-start | bytes 1179656 | tf_op jit(solution)/shard_map/ppermute | solution.py:23
  77.7 1.9 %collective-permute-start.5 = (bf16[8,2,32,384]{3,2,1,0:T(8,128)(2,1)S(1)}, bf16[8,2,32,384]{3,2,1,0:T(8,128)(2,1)S(1)}, u32[]{:S(2)}, u32[]{:S(2)}) collective-permute-start(bf16[8,2,32,384]{3,2,1,0:T(8,128)(2,1)S(1)} %collective-permute-done.3.refs_1_), channel_id=1, source_target_pairs={{0,8},{8,0},{16,24},{24,16},{32,40},{40,32},{48,56},{56,48},{64,72... | collective-permute-start | bytes 1179656 | tf_op jit(solution)/shard_map/ppermute | solution.py:23
  79.6 0.0 collective-permute-done.6
  79.7 2.4 %collective-permute-start.7 = (bf16[8,2,32,384]{3,2,1,0:T(8,128)(2,1)S(1)}, bf16[8,2,32,384]{3,2,1,0:T(8,128)(2,1)S(1)}, u32[]{:S(2)}, u32[]{:S(2)}) collective-permute-start(bf16[8,2,32,384]{3,2,1,0:T(8,128)(2,1)S(1)} %collective-permute-done.6), channel_id=1, source_target_pairs={{0,8},{8,0},{16,24},{24,16},{32,40},{40,32},{48,56},{56,48},{64,72... | collective-permute-start | bytes 1179656 | tf_op jit(solution)/shard_map/ppermute | solution.py:23
  82.1 0.1 pad_add_fusion.reach
  82.2 0.0 collective-permute-done.4.refs_3_
  82.2 4.8 %own_and_near.1 = (f32[3,256,128]{2,1,0:T(8,128)S(1)}, f32[3,256,128]{2,1,0:T(8,128)S(1)}, f32[3,256,128]{2,1,0:T(8,128)S(1)}) custom-call(s32[8]{0:T(128)S(1)} %pad_add_fusion.reach, bf16[8,32,384]{2,1,0:T(8,128)(2,1)S(1)} %all-to-all-done.1.queries, bf16[8,2,32,384]{3,2,1,0:T(8,128)(2,1)S(1)} %all_to_all.15.own, ...), custom_call_target="tpu_custom_call" | custom-call | flops 1000000000 | bytes 6000000 | tf_op jit(solution)/shard_map/own_and_near/pallas_call | solution.py:155
  87.0 0.0 collective-permute-done.8.refs_3_
  87.0 0.0 collective-permute-done.5.refs_0_
  87.0 0.0 collective-permute-done.7.refs_1_
  87.0 2.5 %far_and_merge.1 = bf16[8,32,384]{2,1,0:T(8,128)(2,1)S(1)} custom-call(s32[8]{0:T(128)S(1)} %pad_add_fusion.reach, bf16[8,32,384]{2,1,0:T(8,128)(2,1)S(1)} %all-to-all-done.1.queries, f32[3,256,128]{2,1,0:T(8,128)S(1)} %get-tuple-element.13.top_in, f32[3,256,128]{2,1,0:T(8,128)S(1)} %get-tuple-element.14.sum_in, ...), custom_call_target="tpu_custom_call" | custom-call | flops 2000000000 | bytes 4000000 | tf_op jit(solution)/shard_map/far_and_merge/pallas_call | solution.py:171
  89.5 16.1 %all_to_all.16 = bf16[8,32,384]{2,1,0:T(8,128)(2,1)S(1)} all-to-all(bf16[8,32,384]{2,1,0:T(8,128)(2,1)S(1)} %far_and_merge.1), channel_id=1, replica_groups=mesh['frame'=64,'space'=8] {'space'}, dimensions={0} | all-to-all | bytes 393216 | tf_op jit(solution)/shard_map/all_to_all | solution.py:219
  105.6 0.1 copy.7
  105.6 0.8 reshape.7
  (3 shorter events, 0.1 us)
Async XLA Ops:
  1.1 48.8 %copy-start = (bf16[1,32,3072]{2,1,0:T(8,128)(2,1)S(1)}, bf16[1,32,3072]{2,1,0:T(8,128)(2,1)}, u32[]{:S(2)}) copy-start(bf16[1,32,3072]{2,1,0:T(8,128)(2,1)} %param.4) | copy-start | bytes 589828
  25.4 5.4 %collective-permute-start.2 = (bf16[8,2,32,384]{3,2,1,0:T(8,128)(2,1)S(1)}, bf16[8,2,32,384]{3,2,1,0:T(8,128)(2,1)S(1)}, u32[]{:S(2)}, u32[]{:S(2)}) collective-permute-start(bf16[8,2,32,384]{3,2,1,0:T(8,128)(2,1)S(1)} %all_to_all.15.own), channel_id=1, source_target_pairs={{0,8},{8,0},{16,24},{24,16},{32,40},{40,32},{48,56},{56,48},{64,72... | collective-permute-start | bytes 1179656 | tf_op jit(solution)/shard_map/ppermute | solution.py:23
  30.8 13.8 %collective-permute-start.3 = (bf16[8,2,32,384]{3,2,1,0:T(8,128)(2,1)S(1)}, bf16[8,2,32,384]{3,2,1,0:T(8,128)(2,1)S(1)}, u32[]{:S(2)}, u32[]{:S(2)}) collective-permute-start(bf16[8,2,32,384]{3,2,1,0:T(8,128)(2,1)S(1)} %collective-permute-done.2.refs_0_), channel_id=1, source_target_pairs={{0,16},{8,504},{16,32},{24,8},{32,48},{40,24},{48,64},{56,40},{64,... | collective-permute-start | bytes 1179656 | tf_op jit(solution)/shard_map/ppermute | solution.py:23
  38.1 25.8 %collective-permute-start.1 = (bf16[8,2,32,384]{3,2,1,0:T(8,128)(2,1)S(1)}, bf16[8,2,32,384]{3,2,1,0:T(8,128)(2,1)S(1)}, u32[]{:S(2)}, u32[]{:S(2)}) collective-permute-start(bf16[8,2,32,384]{3,2,1,0:T(8,128)(2,1)S(1)} %all_to_all.15.own), channel_id=1, source_target_pairs={{0,16},{8,504},{16,32},{24,8},{32,48},{40,24},{48,64},{56,40},{64,... | collective-permute-start | bytes 1179656 | tf_op jit(solution)/shard_map/ppermute | solution.py:23
  41.1 33.5 %collective-permute-start = (bf16[8,2,32,384]{3,2,1,0:T(8,128)(2,1)S(1)}, bf16[8,2,32,384]{3,2,1,0:T(8,128)(2,1)S(1)}, u32[]{:S(2)}, u32[]{:S(2)}) collective-permute-start(bf16[8,2,32,384]{3,2,1,0:T(8,128)(2,1)S(1)} %all_to_all.15.own), channel_id=1, source_target_pairs={{0,64},{8,456},{16,80},{24,472},{32,96},{40,488},{48,112},{56,504}... | collective-permute-start | bytes 1179656 | tf_op jit(solution)/shard_map/ppermute | solution.py:23
  44.6 35.0 %collective-permute-start.6 = (bf16[8,2,32,384]{3,2,1,0:T(8,128)(2,1)S(1)}, bf16[8,2,32,384]{3,2,1,0:T(8,128)(2,1)S(1)}, u32[]{:S(2)}, u32[]{:S(2)}) collective-permute-start(bf16[8,2,32,384]{3,2,1,0:T(8,128)(2,1)S(1)} %collective-permute-done.3.refs_1_), channel_id=1, source_target_pairs={{0,16},{8,504},{16,32},{24,8},{32,48},{40,24},{48,64},{56,40},{64,... | collective-permute-start | bytes 1179656 | tf_op jit(solution)/shard_map/ppermute | solution.py:23
  63.9 11.9 %all-to-all-start.1 = ((bf16[8,32,384]{2,1,0:T(8,128)(2,1)}), bf16[8,32,384]{2,1,0:T(8,128)(2,1)S(1)}, u32[]{:S(2)}, u32[]{:S(2)}) async-start(bf16[8,32,384]{2,1,0:T(8,128)(2,1)} %bitcast.25), calls=%async_computation.1 | async-start | bytes 393216 | tf_op jit(solution)/shard_map/all_to_all | solution.py:211
  67.3 7.2 %copy-start.1 = (s32[1,8]{1,0:T(1,128)S(1)}, s32[1,8]{1,0:T(1,128)}, u32[]{:S(2)}) copy-start(s32[1,8]{1,0:T(1,128)} %param.7) | copy-start | bytes 100
  67.3 14.9 %collective-permute-start.4 = (bf16[8,2,32,384]{3,2,1,0:T(8,128)(2,1)S(1)}, bf16[8,2,32,384]{3,2,1,0:T(8,128)(2,1)S(1)}, u32[]{:S(2)}, u32[]{:S(2)}) collective-permute-start(bf16[8,2,32,384]{3,2,1,0:T(8,128)(2,1)S(1)} %collective-permute-done.1.refs_2_), channel_id=1, source_target_pairs={{0,16},{8,504},{16,32},{24,8},{32,48},{40,24},{48,64},{56,40},{64,... | collective-permute-start | bytes 1179656 | tf_op jit(solution)/shard_map/ppermute | solution.py:23
  75.8 11.2 %collective-permute-start.8 = (bf16[8,2,32,384]{3,2,1,0:T(8,128)(2,1)S(1)}, bf16[8,2,32,384]{3,2,1,0:T(8,128)(2,1)S(1)}, u32[]{:S(2)}, u32[]{:S(2)}) collective-permute-start(bf16[8,2,32,384]{3,2,1,0:T(8,128)(2,1)S(1)} %collective-permute-done.refs_2_), channel_id=1, source_target_pairs={{0,384},{8,136},{16,400},{24,152},{32,416},{40,168},{48,432},{56,1... | collective-permute-start | bytes 1179656 | tf_op jit(solution)/shard_map/ppermute | solution.py:23
  77.7 9.3 %collective-permute-start.5 = (bf16[8,2,32,384]{3,2,1,0:T(8,128)(2,1)S(1)}, bf16[8,2,32,384]{3,2,1,0:T(8,128)(2,1)S(1)}, u32[]{:S(2)}, u32[]{:S(2)}) collective-permute-start(bf16[8,2,32,384]{3,2,1,0:T(8,128)(2,1)S(1)} %collective-permute-done.3.refs_1_), channel_id=1, source_target_pairs={{0,8},{8,0},{16,24},{24,16},{32,40},{40,32},{48,56},{56,48},{64,72... | collective-permute-start | bytes 1179656 | tf_op jit(solution)/shard_map/ppermute | solution.py:23
  79.7 7.3 %collective-permute-start.7 = (bf16[8,2,32,384]{3,2,1,0:T(8,128)(2,1)S(1)}, bf16[8,2,32,384]{3,2,1,0:T(8,128)(2,1)S(1)}, u32[]{:S(2)}, u32[]{:S(2)}) collective-permute-start(bf16[8,2,32,384]{3,2,1,0:T(8,128)(2,1)S(1)} %collective-permute-done.6), channel_id=1, source_target_pairs={{0,8},{8,0},{16,24},{24,16},{32,40},{40,32},{48,56},{56,48},{64,72... | collective-permute-start | bytes 1179656 | tf_op jit(solution)/shard_map/ppermute | solution.py:23

commit v3 on v1

--- a/solution.py
+++ b/solution.py
@@ -40,7 +40,7 @@
 
 
 def rows_of(ref, part, at, start=0, count=None):
-    whole = ref[:, part, :, at] if part is not None else ref[:, :, at]
+    whole = ref[:, part, :, at]
     whole = whole.reshape(whole.shape[0] * whole.shape[1], HD)
     return whole if count is None else whole[start : start + count]
 
@@ -76,15 +76,39 @@
     return jnp.concatenate([w.astype(jnp.bfloat16) for w in weights], 1), total
 
 
+def split_kernel(pair, queries, out):
+    wide = out.shape[-1]
+    for share in range(out.shape[0]):
+        at = slice(share * wide, (share + 1) * wide)
+        out[share, 0] = pair[0, :, at]
+        out[share, 1] = pair[1, :, at]
+        out[share, 2] = queries[0, :, at]
+
+
+def split_call(pair, queries, space):
+    _, rows, feat = pair.shape
+    return pl.pallas_call(
+        split_kernel,
+        in_specs=[pl.BlockSpec(memory_space=pltpu.VMEM)] * 2,
+        out_specs=pl.BlockSpec(memory_space=pltpu.VMEM),
+        out_shape=jax.ShapeDtypeStruct((space, 3, rows, feat // space), pair.dtype),
+        compiler_params=pltpu.CompilerParams(vmem_limit_bytes=vmem_bytes),
+        cost_estimate=pl.CostEstimate(
+            flops=20_000_000_000, bytes_accessed=1_200_000, transcendentals=0
+        ),
+        name="heads_apart",
+    )(pair, queries)
+
+
 def near_kernel(frame_rows, columns, scale, reach, queries, own, *refs):
     partner_refs = refs[: len(columns)]
     top_out, sum_out, product_out = refs[len(columns) :]
     lean = row_gap()
     limits = [reach[column] for column in columns]
     blocks = range(frame_rows // Q_ROWS)
-    for head in range(queries.shape[2] // HD):
+    for head in range(own.shape[3] // HD):
         at = slice(head * HD, (head + 1) * HD)
-        all_queries = rows_of(queries, None, at)
+        all_queries = rows_of(queries, 2, at)
         own_keys = rows_of(own, 0, at)
         own_values = rows_of(own, 1, at)
         for block in blocks:
@@ -112,9 +136,9 @@
     parts = Q_ROWS // out.shape[1]
     blocks = range(frame_rows // Q_ROWS)
     span = [slice(block * Q_ROWS, (block + 1) * Q_ROWS) for block in blocks]
-    for head in range(queries.shape[2] // HD):
+    for head in range(queries.shape[3] // HD):
         at = slice(head * HD, (head + 1) * HD)
-        all_queries = rows_of(queries, None, at)
+        all_queries = rows_of(queries, 2, at)
         tiles = [
             banded(all_queries[span[b]], b, frame_rows, limits, partner_refs, at, lean, scale)
             for b in blocks
@@ -150,7 +174,7 @@
 
 
 def near_call(reach, queries, own, partners, columns, scale):
-    space, rows, feat = queries.shape
+    space, _, rows, feat = own.shape
     state = jax.ShapeDtypeStruct((feat // HD, space * rows, HD), jnp.float32)
     return pl.pallas_call(
         functools.partial(near_kernel, space * rows, columns, scale),
@@ -167,7 +191,7 @@
 
 
 def far_call(reach, queries, state, partners, columns, scale):
-    space, rows, feat = queries.shape
+    space, _, rows, feat = queries.shape
     return pl.pallas_call(
         functools.partial(far_kernel, space * rows, columns, scale),
         in_specs=[pl.BlockSpec(memory_space=pltpu.SMEM)]
@@ -187,7 +211,6 @@
     space = lax.axis_size("space")
     frame_pos = lax.axis_index("frame")
     frame_count = lax.axis_size("frame")
-    wide = feat // space
 
     distance = 2 ** jnp.arange(OCTAVES, dtype=jnp.int32)
     below = jnp.where(frame_pos - distance >= 0, windows[0, 0::2], -1)
@@ -195,28 +218,28 @@
     upper = ((frame_pos & 1) == 0) == (distance == 1)
     reach = jnp.concatenate([jnp.where(upper, above, below), jnp.where(upper, below, above)])
 
-    pair = jnp.stack([keys[0], values[0]]).reshape(2, rows, space, wide)
-    own = lax.all_to_all(jnp.transpose(pair, (2, 0, 1, 3)), "space", 0, 0, tiled=True)
-
-    split = jnp.transpose(queries[0].reshape(rows, space, wide), (1, 0, 2))
-    first_eight = crossed(own, 8, 1)
+    pair = jnp.concatenate([keys, values], 0)
+    far_rows = crossed(pair, 8, 1)
+    shares = jnp.transpose(pair.reshape(2, rows, space, feat // space), (2, 0, 1, 3))
+    own = lax.all_to_all(shares, "space", 0, 0, tiled=True)
+
     first_two = crossed(own, 2, 1)
     second_two = crossed(own, 2, -1)
-    first_one = crossed(own, 1, 1)
-    split = lax.all_to_all(split, "space", 0, 0, tiled=True)
-    first_two, second_two, split = lax.optimization_barrier((first_two, second_two, split))
+    first_two, second_two, whole = lax.optimization_barrier(
+        (first_two, second_two, split_call(far_rows, queries, space))
+    )
+    whole = lax.all_to_all(whole, "space", 0, 0, tiled=True)
     first_four = crossed(first_two, 2, 1)
     second_four = crossed(second_two, 2, -1)
-    own_late, _ = lax.optimization_barrier((own, first_two))
+    second_eight = crossed(whole[:, :2], 16, -1)
+    own_late, _ = lax.optimization_barrier((own, (first_two, second_two)))
+    first_one = crossed(own_late, 1, 1)
     second_one = crossed(own_late, 1, -1)
-    second_eight = crossed(first_eight, 16, -1)
-
-    near = [first_one, second_one, first_two, second_two]
-    state = near_call(reach, split, own, near, [0, 4, 1, 5], scale)
-    far = [first_four, second_four, first_eight, second_eight]
-    result = far_call(
-        reach, split, state, far, [2, 6, 3, 7], scale
-    )
+
+    near = [first_two, second_two, first_four, second_four]
+    state = near_call(reach, whole, own, near, [1, 5, 2, 6], scale)
+    far = [first_one, second_one, whole, second_eight]
+    result = far_call(reach, whole, state, far, [0, 4, 3, 7], scale)
     result = lax.all_to_all(result, "space", 0, 0, tiled=True)
     return jnp.transpose(result, (1, 0, 2)).reshape(1, rows, feat)
 

time: 98.2 us -> 105 us (1.069)
  blocking collectives: 38.9 us -> 16.3 us
  starting transfers between devices: 37.2 us -> 52.3 us
  waiting for transfers between devices: 11 us -> 24.5 us
  local copies, waits for them, and re-layouts: 1.81 us -> 2.92 us
    all_to_all x1 -> x0, blocking collectives: 24.3 us -> none  [heads_plan(): lax.all_to_all(jnp.transpose(pair, (2, 0, 1, 3)), 'space', 0, 0, tiled=True)]
    all_to_all x1 -> x2, starting transfers between devices: 3.39 us -> 17.8 us  [the longest x1 11 us: heads_plan(): own = lax.all_to_all(shares, 'space', 0, 0, tiled=True)]
    all_to_all x1 -> x2, waiting for transfers between devices: 0.01 us -> 10 us  [the longest x1 5.46 us: heads_plan(): whole = lax.all_to_all(whole, 'space', 0, 0, tiled=True)]
    ppermute x8, waiting for transfers between devices: 11 us -> 14.4 us  [crossed(): lax.ppermute(array, 'frame', [(i, (i + by * s) % length) for i, s in enum...]
    all_to_all x1, blocking collectives: 14.6 us -> 16.3 us  [heads_plan(): result = lax.all_to_all(result, 'space', 0, 0, tiled=True)]
    another operation x1 -> x0, other arithmetic: 1.06 us -> none  [heads_plan(): pair = jnp.stack([keys[0], values[0]]).reshape(2, rows, space, wide)]
  transfers between devices with their start and end apart: 9 -> 10, of which waited for: 2 -> 6; matrix products, arithmetic and copies ran while one was open for 1% -> 0% of each run, Pallas kernels for 5% -> 5%
where the time goes in v3:
time: 105 us; the launch traced here: 104 us
  starting transfers between devices  52.3 us (50%)
  waiting for transfers between devices  24.5 us (23%)
  blocking collectives  16.3 us (16%)
  Pallas kernels  8.11 us (8%)
  local copies, waits for them, and re-layouts  2.92 us (3%)
    ppermute x8, starting transfers between devices, crossed(): lax.ppermute(array, 'frame', [(i, (i + by * s) % length) for i, s in enum...  34.4 us
    all_to_all x1, blocking collectives, heads_plan(): result = lax.all_to_all(result, 'space', 0, 0, tiled=True)  16.3 us
    ppermute x8, waiting for transfers between devices, crossed(): lax.ppermute(array, 'frame', [(i, (i + by * s) % length) for i, s in enum...  14.4 us
    all_to_all x1, starting transfers between devices, heads_plan(): own = lax.all_to_all(shares, 'space', 0, 0, tiled=True)  11 us
    all_to_all x1, starting transfers between devices, heads_plan(): whole = lax.all_to_all(whole, 'space', 0, 0, tiled=True)  6.85 us
    all_to_all x1, waiting for transfers between devices, heads_plan(): whole = lax.all_to_all(whole, 'space', 0, 0, tiled=True)  5.46 us
    pallas_call x1, Pallas kernels, near_call(): pl.pallas_call(functools.partial(near_kernel, space * rows, columns, scal...  4.8 us
    all_to_all x1, waiting for transfers between devices, heads_plan(): own = lax.all_to_all(shares, 'space', 0, 0, tiled=True)  4.55 us
  transfers between devices with their start and end apart: 10, of which 6 were waited for; matrix products, arithmetic and copies ran while one was open for 0% of the time, Pallas kernels for 5%

profile of v3, /device:TPU:1, one launch (start us, length us, event | category | flops | bytes accessed | tf_op | source)
XLA Modules:
  0.0 104.3 jit_solution(3698140449576156164)
XLA Ops:
  0.0 0.0 copy-start.1
  0.0 1.0 constant_dynamic-update-slice_fusion.1
  1.0 0.0 copy-done.1
  1.0 0.8 copy.9
  1.8 0.0 copy-start
  1.8 11.0 %all-to-all-start = ((bf16[8,2,32,384]{3,2,1,0:T(8,128)(2,1)}), bf16[8,2,32,384]{3,2,1,0:T(8,128)(2,1)S(1)}, u32[]{:S(2)}, u32[]{:S(2)}) async-start(bf16[8,2,32,384]{3,2,1,0:T(8,128)(2,1)} %bitcast.19), calls=%async_computation | async-start | bytes 786432 | tf_op jit(solution)/shard_map/all_to_all | solution.py:224
  12.8 9.6 %collective-permute-start.2 = (bf16[2,32,3072]{2,1,0:T(8,128)(2,1)S(1)}, bf16[2,32,3072]{2,1,0:T(8,128)(2,1)S(1)}, u32[]{:S(2)}, u32[]{:S(2)}) collective-permute-start(bf16[2,32,3072]{2,1,0:T(8,128)(2,1)S(1)} %constant_dynamic-update-slice_fusion), channel_id=1, source_target_pairs={{0,64},{8,456},{16,80},{24,472},{32,96},{40,488},{48,112},{56,504}... | collective-permute-start | bytes 1179656 | tf_op jit(solution)/shard_map/ppermute | solution.py:23
  22.5 4.6 %all-to-all-done.own = bf16[8,2,32,384]{3,2,1,0:T(8,128)(2,1)S(1)} async-done(((bf16[8,2,32,384]{3,2,1,0:T(8,128)(2,1)}), bf16[8,2,32,384]{3,2,1,0:T(8,128)(2,1)S(1)}, u32[]{:S(2)}, u32[]{:S(2)}) %all-to-all-start) | async-done | bytes 393248 | tf_op jit(solution)/shard_map/all_to_all | solution.py:224
  27.0 7.3 %collective-permute-start = (bf16[8,2,32,384]{3,2,1,0:T(8,128)(2,1)S(1)}, bf16[8,2,32,384]{3,2,1,0:T(8,128)(2,1)S(1)}, u32[]{:S(2)}, u32[]{:S(2)}) collective-permute-start(bf16[8,2,32,384]{3,2,1,0:T(8,128)(2,1)S(1)} %all-to-all-done.own), channel_id=1, source_target_pairs={{0,16},{8,504},{16,32},{24,8},{32,48},{40,24},{48,64},{56,40},{64,... | collective-permute-start | bytes 1179656 | tf_op jit(solution)/shard_map/ppermute | solution.py:23
  34.3 1.9 %collective-permute-start.1 = (bf16[8,2,32,384]{3,2,1,0:T(8,128)(2,1)S(1)}, bf16[8,2,32,384]{3,2,1,0:T(8,128)(2,1)S(1)}, u32[]{:S(2)}, u32[]{:S(2)}) collective-permute-start(bf16[8,2,32,384]{3,2,1,0:T(8,128)(2,1)S(1)} %all-to-all-done.own), channel_id=1, source_target_pairs={{0,496},{8,24},{16,0},{24,40},{32,16},{40,56},{48,32},{56,72},{64,... | collective-permute-start | bytes 1179656 | tf_op jit(solution)/shard_map/ppermute | solution.py:23
  36.3 3.6 %collective-permute-done.2.pair = bf16[2,32,3072]{2,1,0:T(8,128)(2,1)S(1)} collective-permute-done((bf16[2,32,3072]{2,1,0:T(8,128)(2,1)S(1)}, bf16[2,32,3072]{2,1,0:T(8,128)(2,1)S(1)}, u32[]{:S(2)}, u32[]{:S(2)}) %collective-permute-start.2) | collective-permute-done | bytes 393248 | tf_op jit(solution)/shard_map/ppermute | solution.py:23
  39.8 0.0 copy-done
  39.8 0.9 heads_apart.1
  40.7 7.7 %collective-permute-done.refs_0_ = bf16[8,2,32,384]{3,2,1,0:T(8,128)(2,1)S(1)} collective-permute-done((bf16[8,2,32,384]{3,2,1,0:T(8,128)(2,1)S(1)}, bf16[8,2,32,384]{3,2,1,0:T(8,128)(2,1)S(1)}, u32[]{:S(2)}, u32[]{:S(2)}) %collective-permute-start) | collective-permute-done | bytes 393248 | tf_op jit(solution)/shard_map/ppermute | solution.py:23
  48.4 0.4 collective-permute-done.1.refs_1_
  48.7 6.8 %all-to-all-start.1 = ((bf16[8,3,32,384]{3,2,1,0:T(8,128)(2,1)}), bf16[8,3,32,384]{3,2,1,0:T(8,128)(2,1)S(1)}, u32[]{:S(2)}, u32[]{:S(2)}) async-start(bf16[8,3,32,384]{3,2,1,0:T(8,128)(2,1)} %heads_apart.1), calls=%async_computation.1 | async-start | bytes 1179648 | tf_op jit(solution)/shard_map/all_to_all | solution.py:231
  55.6 0.0 copy-start.2
  55.6 6.3 %collective-permute-start.3 = (bf16[8,2,32,384]{3,2,1,0:T(8,128)(2,1)S(1)}, bf16[8,2,32,384]{3,2,1,0:T(8,128)(2,1)S(1)}, u32[]{:S(2)}, u32[]{:S(2)}) collective-permute-start(bf16[8,2,32,384]{3,2,1,0:T(8,128)(2,1)S(1)} %collective-permute-done.refs_0_), channel_id=1, source_target_pairs={{0,16},{8,504},{16,32},{24,8},{32,48},{40,24},{48,64},{56,40},{64,... | collective-permute-start | bytes 1179656 | tf_op jit(solution)/shard_map/ppermute | solution.py:23
  61.9 1.9 %collective-permute-start.4 = (bf16[8,2,32,384]{3,2,1,0:T(8,128)(2,1)S(1)}, bf16[8,2,32,384]{3,2,1,0:T(8,128)(2,1)S(1)}, u32[]{:S(2)}, u32[]{:S(2)}) collective-permute-start(bf16[8,2,32,384]{3,2,1,0:T(8,128)(2,1)S(1)} %collective-permute-done.1.refs_1_), channel_id=1, source_target_pairs={{0,496},{8,24},{16,0},{24,40},{32,16},{40,56},{48,32},{56,72},{64,... | collective-permute-start | bytes 1179656 | tf_op jit(solution)/shard_map/ppermute | solution.py:23
  63.8 0.0 copy-done.2
  63.8 0.1 slice.10
  63.9 0.1 slice.9
  64.0 3.5 %collective-permute-start.5 = (bf16[8,2,32,384]{3,2,1,0:T(8,128)(2,1)S(1)}, bf16[8,2,32,384]{3,2,1,0:T(8,128)(2,1)S(1)}, u32[]{:S(2)}, u32[]{:S(2)}) collective-permute-start(bf16[8,2,32,384]{3,2,1,0:T(8,128)(2,1)S(1)} %all-to-all-done.own), channel_id=1, source_target_pairs={{0,8},{8,0},{16,24},{24,16},{32,40},{40,32},{48,56},{56,48},{64,72... | collective-permute-start | bytes 1179656 | tf_op jit(solution)/shard_map/ppermute | solution.py:23
  67.5 1.9 %collective-permute-start.6 = (bf16[8,2,32,384]{3,2,1,0:T(8,128)(2,1)S(1)}, bf16[8,2,32,384]{3,2,1,0:T(8,128)(2,1)S(1)}, u32[]{:S(2)}, u32[]{:S(2)}) collective-permute-start(bf16[8,2,32,384]{3,2,1,0:T(8,128)(2,1)S(1)} %all-to-all-done.own), channel_id=1, source_target_pairs={{0,504},{8,16},{16,8},{24,32},{32,24},{40,48},{48,40},{56,64},{64,... | collective-permute-start | bytes 1179656 | tf_op jit(solution)/shard_map/ppermute | solution.py:23
  69.5 5.5 %all-to-all-done.1.queries.refs_2_ = bf16[8,3,32,384]{3,2,1,0:T(8,128)(2,1)S(1)} async-done(((bf16[8,3,32,384]{3,2,1,0:T(8,128)(2,1)}), bf16[8,3,32,384]{3,2,1,0:T(8,128)(2,1)S(1)}, u32[]{:S(2)}, u32[]{:S(2)}) %all-to-all-start.1) | async-done | bytes 589856 | tf_op jit(solution)/shard_map/all_to_all | solution.py:231
  75.0 1.9 %collective-permute-start.7 = (bf16[8,2,32,384]{3,2,1,0:T(8,128)(2,1)S(1)}, bf16[8,2,32,384]{3,2,1,0:T(8,128)(2,1)S(1)}, u32[]{:S(2)}, u32[]{:S(2)}) collective-permute-start(bf16[8,2,32,384]{3,2,1,0:T(8,128)(2,1)S(1)} %slice.12), channel_id=1, source_target_pairs={{0,384},{8,136},{16,400},{24,152},{32,416},{40,168},{48,432},{56,1... | collective-permute-start | bytes 1179656 | tf_op jit(solution)/shard_map/ppermute | solution.py:23
  76.9 0.1 pad_add_fusion.reach
  77.0 0.0 collective-permute-done.3.refs_2_
  77.0 0.0 collective-permute-done.4.refs_3_
  77.0 4.8 %own_and_near.1 = (f32[3,256,128]{2,1,0:T(8,128)S(1)}, f32[3,256,128]{2,1,0:T(8,128)S(1)}, f32[3,256,128]{2,1,0:T(8,128)S(1)}) custom-call(s32[8]{0:T(128)S(1)} %pad_add_fusion.reach, bf16[8,3,32,384]{3,2,1,0:T(8,128)(2,1)S(1)} %all-to-all-done.1.queries.refs_2_, bf16[8,2,32,384]{3,2,1,0:T(8,128)(2,1)S(1)} %all-to-all-done.own, ...), custom_call_target="tpu_custom_call" | custom-call | flops 1000000000 | bytes 6000000 | tf_op jit(solution)/shard_map/own_and_near/pallas_call | solution.py:179
  81.8 0.0 collective-permute-done.5.refs_0_
  81.8 0.0 collective-permute-done.6.refs_1_
  81.8 2.9 %collective-permute-done.7.refs_3_ = bf16[8,2,32,384]{3,2,1,0:T(8,128)(2,1)S(1)} collective-permute-done((bf16[8,2,32,384]{3,2,1,0:T(8,128)(2,1)S(1)}, bf16[8,2,32,384]{3,2,1,0:T(8,128)(2,1)S(1)}, u32[]{:S(2)}, u32[]{:S(2)}) %collective-permute-start.7) | collective-permute-done | bytes 393248 | tf_op jit(solution)/shard_map/ppermute | solution.py:23
  84.7 2.4 %far_and_merge.1 = bf16[8,32,384]{2,1,0:T(8,128)(2,1)S(1)} custom-call(s32[8]{0:T(128)S(1)} %pad_add_fusion.reach, bf16[8,3,32,384]{3,2,1,0:T(8,128)(2,1)S(1)} %all-to-all-done.1.queries.refs_2_, f32[3,256,128]{2,1,0:T(8,128)S(1)} %get-tuple-element.15.top_in, f32[3,256,128]{2,1,0:T(8,128)S(1)} %get-tuple-element.16.sum_in, ...), custom_call_target="tpu_custom_call" | custom-call | flops 2000000000 | bytes 4000000 | tf_op jit(solution)/shard_map/far_and_merge/pallas_call | solution.py:195
  87.2 16.3 %all_to_all.15 = bf16[8,32,384]{2,1,0:T(8,128)(2,1)S(1)} all-to-all(bf16[8,32,384]{2,1,0:T(8,128)(2,1)S(1)} %far_and_merge.1), channel_id=1, replica_groups=mesh['frame'=64,'space'=8] {'space'}, dimensions={0} | all-to-all | bytes 393216 | tf_op jit(solution)/shard_map/all_to_all | solution.py:243
  103.4 0.1 copy.6
  103.5 0.8 reshape.7
  (3 shorter events, 0.1 us)
Async XLA Ops:
  0.0 1.0 copy-start.1
  1.8 38.0 %copy-start = (bf16[1,32,3072]{2,1,0:T(8,128)(2,1)S(1)}, bf16[1,32,3072]{2,1,0:T(8,128)(2,1)}, u32[]{:S(2)}) copy-start(bf16[1,32,3072]{2,1,0:T(8,128)(2,1)} %queries.1) | copy-start | bytes 589828
  1.8 25.2 %all-to-all-start = ((bf16[8,2,32,384]{3,2,1,0:T(8,128)(2,1)}), bf16[8,2,32,384]{3,2,1,0:T(8,128)(2,1)S(1)}, u32[]{:S(2)}, u32[]{:S(2)}) async-start(bf16[8,2,32,384]{3,2,1,0:T(8,128)(2,1)} %bitcast.19), calls=%async_computation | async-start | bytes 786432 | tf_op jit(solution)/shard_map/all_to_all | solution.py:224
  12.8 27.0 %collective-permute-start.2 = (bf16[2,32,3072]{2,1,0:T(8,128)(2,1)S(1)}, bf16[2,32,3072]{2,1,0:T(8,128)(2,1)S(1)}, u32[]{:S(2)}, u32[]{:S(2)}) collective-permute-start(bf16[2,32,3072]{2,1,0:T(8,128)(2,1)S(1)} %constant_dynamic-update-slice_fusion), channel_id=1, source_target_pairs={{0,64},{8,456},{16,80},{24,472},{32,96},{40,488},{48,112},{56,504}... | collective-permute-start | bytes 1179656 | tf_op jit(solution)/shard_map/ppermute | solution.py:23
  27.0 21.3 %collective-permute-start = (bf16[8,2,32,384]{3,2,1,0:T(8,128)(2,1)S(1)}, bf16[8,2,32,384]{3,2,1,0:T(8,128)(2,1)S(1)}, u32[]{:S(2)}, u32[]{:S(2)}) collective-permute-start(bf16[8,2,32,384]{3,2,1,0:T(8,128)(2,1)S(1)} %all-to-all-done.own), channel_id=1, source_target_pairs={{0,16},{8,504},{16,32},{24,8},{32,48},{40,24},{48,64},{56,40},{64,... | collective-permute-start | bytes 1179656 | tf_op jit(solution)/shard_map/ppermute | solution.py:23
  34.3 14.4 %collective-permute-start.1 = (bf16[8,2,32,384]{3,2,1,0:T(8,128)(2,1)S(1)}, bf16[8,2,32,384]{3,2,1,0:T(8,128)(2,1)S(1)}, u32[]{:S(2)}, u32[]{:S(2)}) collective-permute-start(bf16[8,2,32,384]{3,2,1,0:T(8,128)(2,1)S(1)} %all-to-all-done.own), channel_id=1, source_target_pairs={{0,496},{8,24},{16,0},{24,40},{32,16},{40,56},{48,32},{56,72},{64,... | collective-permute-start | bytes 1179656 | tf_op jit(solution)/shard_map/ppermute | solution.py:23
  48.7 26.2 %all-to-all-start.1 = ((bf16[8,3,32,384]{3,2,1,0:T(8,128)(2,1)}), bf16[8,3,32,384]{3,2,1,0:T(8,128)(2,1)S(1)}, u32[]{:S(2)}, u32[]{:S(2)}) async-start(bf16[8,3,32,384]{3,2,1,0:T(8,128)(2,1)} %heads_apart.1), calls=%async_computation.1 | async-start | bytes 1179648 | tf_op jit(solution)/shard_map/all_to_all | solution.py:231
  55.6 8.2 %copy-start.2 = (s32[1,8]{1,0:T(1,128)S(1)}, s32[1,8]{1,0:T(1,128)}, u32[]{:S(2)}) copy-start(s32[1,8]{1,0:T(1,128)} %param.7) | copy-start | bytes 100
  55.6 21.4 %collective-permute-start.3 = (bf16[8,2,32,384]{3,2,1,0:T(8,128)(2,1)S(1)}, bf16[8,2,32,384]{3,2,1,0:T(8,128)(2,1)S(1)}, u32[]{:S(2)}, u32[]{:S(2)}) collective-permute-start(bf16[8,2,32,384]{3,2,1,0:T(8,128)(2,1)S(1)} %collective-permute-done.refs_0_), channel_id=1, source_target_pairs={{0,16},{8,504},{16,32},{24,8},{32,48},{40,24},{48,64},{56,40},{64,... | collective-permute-start | bytes 1179656 | tf_op jit(solution)/shard_map/ppermute | solution.py:23
  61.9 15.1 %collective-permute-start.4 = (bf16[8,2,32,384]{3,2,1,0:T(8,128)(2,1)S(1)}, bf16[8,2,32,384]{3,2,1,0:T(8,128)(2,1)S(1)}, u32[]{:S(2)}, u32[]{:S(2)}) collective-permute-start(bf16[8,2,32,384]{3,2,1,0:T(8,128)(2,1)S(1)} %collective-permute-done.1.refs_1_), channel_id=1, source_target_pairs={{0,496},{8,24},{16,0},{24,40},{32,16},{40,56},{48,32},{56,72},{64,... | collective-permute-start | bytes 1179656 | tf_op jit(solution)/shard_map/ppermute | solution.py:23
  64.0 17.8 %collective-permute-start.5 = (bf16[8,2,32,384]{3,2,1,0:T(8,128)(2,1)S(1)}, bf16[8,2,32,384]{3,2,1,0:T(8,128)(2,1)S(1)}, u32[]{:S(2)}, u32[]{:S(2)}) collective-permute-start(bf16[8,2,32,384]{3,2,1,0:T(8,128)(2,1)S(1)} %all-to-all-done.own), channel_id=1, source_target_pairs={{0,8},{8,0},{16,24},{24,16},{32,40},{40,32},{48,56},{56,48},{64,72... | collective-permute-start | bytes 1179656 | tf_op jit(solution)/shard_map/ppermute | solution.py:23
  67.5 14.3 %collective-permute-start.6 = (bf16[8,2,32,384]{3,2,1,0:T(8,128)(2,1)S(1)}, bf16[8,2,32,384]{3,2,1,0:T(8,128)(2,1)S(1)}, u32[]{:S(2)}, u32[]{:S(2)}) collective-permute-start(bf16[8,2,32,384]{3,2,1,0:T(8,128)(2,1)S(1)} %all-to-all-done.own), channel_id=1, source_target_pairs={{0,504},{8,16},{16,8},{24,32},{32,24},{40,48},{48,40},{56,64},{64,... | collective-permute-start | bytes 1179656 | tf_op jit(solution)/shard_map/ppermute | solution.py:23
  75.0 9.7 %collective-permute-start.7 = (bf16[8,2,32,384]{3,2,1,0:T(8,128)(2,1)S(1)}, bf16[8,2,32,384]{3,2,1,0:T(8,128)(2,1)S(1)}, u32[]{:S(2)}, u32[]{:S(2)}) collective-permute-start(bf16[8,2,32,384]{3,2,1,0:T(8,128)(2,1)S(1)} %slice.12), channel_id=1, source_target_pairs={{0,384},{8,136},{16,400},{24,152},{32,416},{40,168},{48,432},{56,1... | collective-permute-start | bytes 1179656 | tf_op jit(solution)/shard_map/ppermute | solution.py:23

commit v4 on v1

--- a/solution.py
+++ b/solution.py
@@ -17,10 +17,20 @@
 vmem_bytes = 40 * 1024 * 1024
 
 
-def crossed(array, by, sense):
+def crossed(array, by, sense, keep=None):
     length = lax.axis_size("frame")
-    signs = [sense if i % 2 == 0 else -sense for i in range(length)]
-    return lax.ppermute(array, "frame", [(i, (i + by * s) % length) for i, s in enumerate(signs)])
+    pairs = []
+    for frame in range(length):
+        target = frame + by * (sense if frame % 2 == 0 else -sense)
+        if keep is None and 0 <= target < length:
+            pairs.append((frame, target))
+        elif keep is not None and keep(target % length, length):
+            pairs.append((frame, target % length))
+    return lax.ppermute(array, "frame", pairs)
+
+
+def has_other_far(frame, length):
+    return frame + 8 < length if frame % 2 == 0 else frame >= 8
 
 
 def dot_nt(left, right):
@@ -199,7 +209,7 @@
     own = lax.all_to_all(jnp.transpose(pair, (2, 0, 1, 3)), "space", 0, 0, tiled=True)
 
     split = jnp.transpose(queries[0].reshape(rows, space, wide), (1, 0, 2))
-    first_eight = crossed(own, 8, 1)
+    first_eight = crossed(own, 8, 1, lambda frame, length: True)
     first_two = crossed(own, 2, 1)
     second_two = crossed(own, 2, -1)
     first_one = crossed(own, 1, 1)
@@ -209,7 +219,7 @@
     second_four = crossed(second_two, 2, -1)
     own_late, _ = lax.optimization_barrier((own, first_two))
     second_one = crossed(own_late, 1, -1)
-    second_eight = crossed(first_eight, 16, -1)
+    second_eight = crossed(first_eight, 16, -1, has_other_far)
 
     near = [first_one, second_one, first_two, second_two]
     state = near_call(reach, split, own, near, [0, 4, 1, 5], scale)

time: 98.2 us -> 97.5 us (level)
  waiting for transfers between devices: 11 us -> 8.1 us
  blocking collectives: 38.9 us -> 41.4 us
    ppermute x8, waiting for transfers between devices: 11 us -> 8.1 us  [crossed(): return lax.ppermute(array, 'frame', pairs)]
    all_to_all x1, blocking collectives: 14.6 us -> 17.1 us  [heads_plan(): result = lax.all_to_all(result, 'space', 0, 0, tiled=True)]
where the time goes in v4:
time: 97.5 us; the launch traced here: 97 us
  blocking collectives  41.4 us (42%)
  starting transfers between devices  37.1 us (38%)
  waiting for transfers between devices  8.1 us (8%)
  Pallas kernels  7.25 us (7%)
  local copies, waits for them, and re-layouts  1.81 us (2%)
  other arithmetic  1.15 us (1%)
    ppermute x8, starting transfers between devices, crossed(): return lax.ppermute(array, 'frame', pairs)  33.7 us
    all_to_all x1, blocking collectives, heads_plan(): lax.all_to_all(jnp.transpose(pair, (2, 0, 1, 3)), 'space', 0, 0, tiled=True)  24.3 us
    all_to_all x1, blocking collectives, heads_plan(): result = lax.all_to_all(result, 'space', 0, 0, tiled=True)  17.1 us
    ppermute x8, waiting for transfers between devices, crossed(): return lax.ppermute(array, 'frame', pairs)  8.1 us
    pallas_call x1, Pallas kernels, near_call(): pl.pallas_call(functools.partial(near_kernel, space * rows, columns, scal...  4.8 us
    all_to_all x1, starting transfers between devices, heads_plan(): split = lax.all_to_all(split, 'space', 0, 0, tiled=True)  3.39 us
    pallas_call x1, Pallas kernels, far_call(): pl.pallas_call(functools.partial(far_kernel, space * rows, columns, scale...  2.45 us
  transfers between devices with their start and end apart: 9, of which 2 were waited for; matrix products, arithmetic and copies ran while one was open for 1% of the time, Pallas kernels for 5%

profile of v4, /device:TPU:1, one launch (start us, length us, event | category | flops | bytes accessed | tf_op | source)
XLA Modules:
  0.0 97.0 jit_solution(12268099960017285076)
XLA Ops:
  0.0 1.1 %pad_maximum_fusion = bf16[2,32,3072]{2,1,0:T(8,128)(2,1)S(1)} fusion(bf16[1,32,3072]{2,1,0:T(8,128)(2,1)} %param.6, bf16[1,32,3072]{2,1,0:T(8,128)(2,1)} %param.5), kind=kLoop, calls=%fused_computation.1 | loop fusion | flops 196608 | bytes 786432 | tf_op jit(solution)/shard_map/stack | solution.py:208
  1.1 0.0 copy-start
  1.1 24.3 %all_to_all.15.own = bf16[8,2,32,384]{3,2,1,0:T(8,128)(2,1)S(1)} all-to-all(bf16[8,2,32,384]{3,2,1,0:T(8,128)(2,1)S(1)} %bitcast.26), channel_id=1, replica_groups=mesh['frame'=64,'space'=8] {'space'}, dimensions={0} | all-to-all | bytes 786432 | tf_op jit(solution)/shard_map/all_to_all | solution.py:209
  25.4 1.3 %collective-permute-start = (bf16[8,2,32,384]{3,2,1,0:T(8,128)(2,1)S(1)}, bf16[8,2,32,384]{3,2,1,0:T(8,128)(2,1)S(1)}, u32[]{:S(2)}, u32[]{:S(2)}) collective-permute-start(bf16[8,2,32,384]{3,2,1,0:T(8,128)(2,1)S(1)} %all_to_all.15.own), channel_id=1, source_target_pairs={{0,16},{16,32},{24,8},{32,48},{40,24},{48,64},{56,40},{64,80},{72,... | collective-permute-start | bytes 1179656 | tf_op jit(solution)/shard_map/ppermute | solution.py:29
  26.7 4.0 %collective-permute-start.1 = (bf16[8,2,32,384]{3,2,1,0:T(8,128)(2,1)S(1)}, bf16[8,2,32,384]{3,2,1,0:T(8,128)(2,1)S(1)}, u32[]{:S(2)}, u32[]{:S(2)}) collective-permute-start(bf16[8,2,32,384]{3,2,1,0:T(8,128)(2,1)S(1)} %all_to_all.15.own), channel_id=1, source_target_pairs={{8,24},{16,0},{24,40},{32,16},{40,56},{48,32},{56,72},{64,48},{72,... | collective-permute-start | bytes 1179656 | tf_op jit(solution)/shard_map/ppermute | solution.py:29
  30.7 0.0 copy-done
  30.8 0.7 copy.13
  31.5 3.4 %all-to-all-start.1 = ((bf16[8,32,384]{2,1,0:T(8,128)(2,1)}), bf16[8,32,384]{2,1,0:T(8,128)(2,1)S(1)}, u32[]{:S(2)}, u32[]{:S(2)}) async-start(bf16[8,32,384]{2,1,0:T(8,128)(2,1)} %bitcast.25), calls=%async_computation.1 | async-start | bytes 393216 | tf_op jit(solution)/shard_map/all_to_all | solution.py:216
  34.9 0.0 copy-start.1
  34.9 9.6 %collective-permute-start.6 = (bf16[8,2,32,384]{3,2,1,0:T(8,128)(2,1)S(1)}, bf16[8,2,32,384]{3,2,1,0:T(8,128)(2,1)S(1)}, u32[]{:S(2)}, u32[]{:S(2)}) collective-permute-start(bf16[8,2,32,384]{3,2,1,0:T(8,128)(2,1)S(1)} %all_to_all.15.own), channel_id=1, source_target_pairs={{0,64},{8,456},{16,80},{24,472},{32,96},{40,488},{48,112},{56,504}... | collective-permute-start | bytes 1179656 | tf_op jit(solution)/shard_map/ppermute | solution.py:29
  44.5 3.9 %collective-permute-start.2 = (bf16[8,2,32,384]{3,2,1,0:T(8,128)(2,1)S(1)}, bf16[8,2,32,384]{3,2,1,0:T(8,128)(2,1)S(1)}, u32[]{:S(2)}, u32[]{:S(2)}) collective-permute-start(bf16[8,2,32,384]{3,2,1,0:T(8,128)(2,1)S(1)} %all_to_all.15.own), channel_id=1, source_target_pairs={{0,8},{8,0},{16,24},{24,16},{32,40},{40,32},{48,56},{56,48},{64,72... | collective-permute-start | bytes 1179656 | tf_op jit(solution)/shard_map/ppermute | solution.py:29
  48.4 0.0 all-to-all-done.1.queries
  48.4 0.0 collective-permute-done.refs_2_
  48.5 0.0 collective-permute-done.1.refs_3_
  48.5 1.9 %collective-permute-start.3 = (bf16[8,2,32,384]{3,2,1,0:T(8,128)(2,1)S(1)}, bf16[8,2,32,384]{3,2,1,0:T(8,128)(2,1)S(1)}, u32[]{:S(2)}, u32[]{:S(2)}) collective-permute-start(bf16[8,2,32,384]{3,2,1,0:T(8,128)(2,1)S(1)} %all_to_all.15.own), channel_id=1, source_target_pairs={{8,16},{16,8},{24,32},{32,24},{40,48},{48,40},{56,64},{64,56},{72,... | collective-permute-start | bytes 1179656 | tf_op jit(solution)/shard_map/ppermute | solution.py:29
  50.4 0.0 copy-done.1
  50.4 0.1 slice.6
  50.5 0.1 slice.7
  50.6 1.3 %collective-permute-start.4 = (bf16[8,2,32,384]{3,2,1,0:T(8,128)(2,1)S(1)}, bf16[8,2,32,384]{3,2,1,0:T(8,128)(2,1)S(1)}, u32[]{:S(2)}, u32[]{:S(2)}) collective-permute-start(bf16[8,2,32,384]{3,2,1,0:T(8,128)(2,1)S(1)} %collective-permute-done.refs_2_), channel_id=1, source_target_pairs={{0,16},{16,32},{24,8},{32,48},{40,24},{48,64},{56,40},{64,80},{72,... | collective-permute-start | bytes 1179656 | tf_op jit(solution)/shard_map/ppermute | solution.py:29
  51.9 4.0 %collective-permute-start.5 = (bf16[8,2,32,384]{3,2,1,0:T(8,128)(2,1)S(1)}, bf16[8,2,32,384]{3,2,1,0:T(8,128)(2,1)S(1)}, u32[]{:S(2)}, u32[]{:S(2)}) collective-permute-start(bf16[8,2,32,384]{3,2,1,0:T(8,128)(2,1)S(1)} %collective-permute-done.1.refs_3_), channel_id=1, source_target_pairs={{8,24},{16,0},{24,40},{32,16},{40,56},{48,32},{56,72},{64,48},{72,... | collective-permute-start | bytes 1179656 | tf_op jit(solution)/shard_map/ppermute | solution.py:29
  55.9 0.0 collective-permute-done.6.refs_2_
  55.9 7.7 %collective-permute-start.7 = (bf16[8,2,32,384]{3,2,1,0:T(8,128)(2,1)S(1)}, bf16[8,2,32,384]{3,2,1,0:T(8,128)(2,1)S(1)}, u32[]{:S(2)}, u32[]{:S(2)}) collective-permute-start(bf16[8,2,32,384]{3,2,1,0:T(8,128)(2,1)S(1)} %collective-permute-done.6.refs_2_), channel_id=1, source_target_pairs={{0,384},{8,136},{16,400},{24,152},{32,416},{40,168},{48,432},{56,1... | collective-permute-start | bytes 1179656 | tf_op jit(solution)/shard_map/ppermute | solution.py:29
  63.6 0.1 pad_add_fusion.reach
  63.7 0.0 collective-permute-done.2.refs_0_
  63.7 7.3 %collective-permute-done.3.refs_1_ = bf16[8,2,32,384]{3,2,1,0:T(8,128)(2,1)S(1)} collective-permute-done((bf16[8,2,32,384]{3,2,1,0:T(8,128)(2,1)S(1)}, bf16[8,2,32,384]{3,2,1,0:T(8,128)(2,1)S(1)}, u32[]{:S(2)}, u32[]{:S(2)}) %collective-permute-start.3) | collective-permute-done | bytes 393248 | tf_op jit(solution)/shard_map/ppermute | solution.py:29
  71.1 4.8 %own_and_near.1 = (f32[3,256,128]{2,1,0:T(8,128)S(1)}, f32[3,256,128]{2,1,0:T(8,128)S(1)}, f32[3,256,128]{2,1,0:T(8,128)S(1)}) custom-call(s32[8]{0:T(128)S(1)} %pad_add_fusion.reach, bf16[8,32,384]{2,1,0:T(8,128)(2,1)S(1)} %all-to-all-done.1.queries, bf16[8,2,32,384]{3,2,1,0:T(8,128)(2,1)S(1)} %all_to_all.15.own, ...), custom_call_target="tpu_custom_call" | custom-call | flops 1000000000 | bytes 6000000 | tf_op jit(solution)/shard_map/own_and_near/pallas_call | solution.py:165
  75.9 0.0 collective-permute-done.4.refs_0_
  75.9 0.0 collective-permute-done.5.refs_1_
  75.9 0.7 collective-permute-done.7.refs_3_
  76.6 2.4 %far_and_merge.1 = bf16[8,32,384]{2,1,0:T(8,128)(2,1)S(1)} custom-call(s32[8]{0:T(128)S(1)} %pad_add_fusion.reach, bf16[8,32,384]{2,1,0:T(8,128)(2,1)S(1)} %all-to-all-done.1.queries, f32[3,256,128]{2,1,0:T(8,128)S(1)} %get-tuple-element.16.top_in, f32[3,256,128]{2,1,0:T(8,128)S(1)} %get-tuple-element.17.sum_in, ...), custom_call_target="tpu_custom_call" | custom-call | flops 2000000000 | bytes 4000000 | tf_op jit(solution)/shard_map/far_and_merge/pallas_call | solution.py:181
  79.1 17.1 %all_to_all.16 = bf16[8,32,384]{2,1,0:T(8,128)(2,1)S(1)} all-to-all(bf16[8,32,384]{2,1,0:T(8,128)(2,1)S(1)} %far_and_merge.1), channel_id=1, replica_groups=mesh['frame'=64,'space'=8] {'space'}, dimensions={0} | all-to-all | bytes 393216 | tf_op jit(solution)/shard_map/all_to_all | solution.py:230
  96.2 0.1 copy.7
  96.3 0.8 reshape.7
  (3 shorter events, 0.1 us)
Async XLA Ops:
  1.1 29.6 %copy-start = (bf16[1,32,3072]{2,1,0:T(8,128)(2,1)S(1)}, bf16[1,32,3072]{2,1,0:T(8,128)(2,1)}, u32[]{:S(2)}) copy-start(bf16[1,32,3072]{2,1,0:T(8,128)(2,1)} %param.4) | copy-start | bytes 589828
  25.4 23.0 %collective-permute-start = (bf16[8,2,32,384]{3,2,1,0:T(8,128)(2,1)S(1)}, bf16[8,2,32,384]{3,2,1,0:T(8,128)(2,1)S(1)}, u32[]{:S(2)}, u32[]{:S(2)}) collective-permute-start(bf16[8,2,32,384]{3,2,1,0:T(8,128)(2,1)S(1)} %all_to_all.15.own), channel_id=1, source_target_pairs={{0,16},{16,32},{24,8},{32,48},{40,24},{48,64},{56,40},{64,80},{72,... | collective-permute-start | bytes 1179656 | tf_op jit(solution)/shard_map/ppermute | solution.py:29
  26.7 21.7 %collective-permute-start.1 = (bf16[8,2,32,384]{3,2,1,0:T(8,128)(2,1)S(1)}, bf16[8,2,32,384]{3,2,1,0:T(8,128)(2,1)S(1)}, u32[]{:S(2)}, u32[]{:S(2)}) collective-permute-start(bf16[8,2,32,384]{3,2,1,0:T(8,128)(2,1)S(1)} %all_to_all.15.own), channel_id=1, source_target_pairs={{8,24},{16,0},{24,40},{32,16},{40,56},{48,32},{56,72},{64,48},{72,... | collective-permute-start | bytes 1179656 | tf_op jit(solution)/shard_map/ppermute | solution.py:29
  31.5 16.9 %all-to-all-start.1 = ((bf16[8,32,384]{2,1,0:T(8,128)(2,1)}), bf16[8,32,384]{2,1,0:T(8,128)(2,1)S(1)}, u32[]{:S(2)}, u32[]{:S(2)}) async-start(bf16[8,32,384]{2,1,0:T(8,128)(2,1)} %bitcast.25), calls=%async_computation.1 | async-start | bytes 393216 | tf_op jit(solution)/shard_map/all_to_all | solution.py:216
  34.9 15.5 %copy-start.1 = (s32[1,8]{1,0:T(1,128)S(1)}, s32[1,8]{1,0:T(1,128)}, u32[]{:S(2)}) copy-start(s32[1,8]{1,0:T(1,128)} %param.7) | copy-start | bytes 100
  34.9 21.0 %collective-permute-start.6 = (bf16[8,2,32,384]{3,2,1,0:T(8,128)(2,1)S(1)}, bf16[8,2,32,384]{3,2,1,0:T(8,128)(2,1)S(1)}, u32[]{:S(2)}, u32[]{:S(2)}) collective-permute-start(bf16[8,2,32,384]{3,2,1,0:T(8,128)(2,1)S(1)} %all_to_all.15.own), channel_id=1, source_target_pairs={{0,64},{8,456},{16,80},{24,472},{32,96},{40,488},{48,112},{56,504}... | collective-permute-start | bytes 1179656 | tf_op jit(solution)/shard_map/ppermute | solution.py:29
  44.5 19.2 %collective-permute-start.2 = (bf16[8,2,32,384]{3,2,1,0:T(8,128)(2,1)S(1)}, bf16[8,2,32,384]{3,2,1,0:T(8,128)(2,1)S(1)}, u32[]{:S(2)}, u32[]{:S(2)}) collective-permute-start(bf16[8,2,32,384]{3,2,1,0:T(8,128)(2,1)S(1)} %all_to_all.15.own), channel_id=1, source_target_pairs={{0,8},{8,0},{16,24},{24,16},{32,40},{40,32},{48,56},{56,48},{64,72... | collective-permute-start | bytes 1179656 | tf_op jit(solution)/shard_map/ppermute | solution.py:29
  48.5 22.6 %collective-permute-start.3 = (bf16[8,2,32,384]{3,2,1,0:T(8,128)(2,1)S(1)}, bf16[8,2,32,384]{3,2,1,0:T(8,128)(2,1)S(1)}, u32[]{:S(2)}, u32[]{:S(2)}) collective-permute-start(bf16[8,2,32,384]{3,2,1,0:T(8,128)(2,1)S(1)} %all_to_all.15.own), channel_id=1, source_target_pairs={{8,16},{16,8},{24,32},{32,24},{40,48},{48,40},{56,64},{64,56},{72,... | collective-permute-start | bytes 1179656 | tf_op jit(solution)/shard_map/ppermute | solution.py:29
  50.6 25.3 %collective-permute-start.4 = (bf16[8,2,32,384]{3,2,1,0:T(8,128)(2,1)S(1)}, bf16[8,2,32,384]{3,2,1,0:T(8,128)(2,1)S(1)}, u32[]{:S(2)}, u32[]{:S(2)}) collective-permute-start(bf16[8,2,32,384]{3,2,1,0:T(8,128)(2,1)S(1)} %collective-permute-done.refs_2_), channel_id=1, source_target_pairs={{0,16},{16,32},{24,8},{32,48},{40,24},{48,64},{56,40},{64,80},{72,... | collective-permute-start | bytes 1179656 | tf_op jit(solution)/shard_map/ppermute | solution.py:29
  51.9 24.0 %collective-permute-start.5 = (bf16[8,2,32,384]{3,2,1,0:T(8,128)(2,1)S(1)}, bf16[8,2,32,384]{3,2,1,0:T(8,128)(2,1)S(1)}, u32[]{:S(2)}, u32[]{:S(2)}) collective-permute-start(bf16[8,2,32,384]{3,2,1,0:T(8,128)(2,1)S(1)} %collective-permute-done.1.refs_3_), channel_id=1, source_target_pairs={{8,24},{16,0},{24,40},{32,16},{40,56},{48,32},{56,72},{64,48},{72,... | collective-permute-start | bytes 1179656 | tf_op jit(solution)/shard_map/ppermute | solution.py:29
  55.9 20.7 %collective-permute-start.7 = (bf16[8,2,32,384]{3,2,1,0:T(8,128)(2,1)S(1)}, bf16[8,2,32,384]{3,2,1,0:T(8,128)(2,1)S(1)}, u32[]{:S(2)}, u32[]{:S(2)}) collective-permute-start(bf16[8,2,32,384]{3,2,1,0:T(8,128)(2,1)S(1)} %collective-permute-done.6.refs_2_), channel_id=1, source_target_pairs={{0,384},{8,136},{16,400},{24,152},{32,416},{40,168},{48,432},{56,1... | collective-permute-start | bytes 1179656 | tf_op jit(solution)/shard_map/ppermute | solution.py:29

commit v5 on v4

--- a/solution.py
+++ b/solution.py
@@ -221,12 +221,10 @@
     second_one = crossed(own_late, 1, -1)
     second_eight = crossed(first_eight, 16, -1, has_other_far)
 
-    near = [first_one, second_one, first_two, second_two]
-    state = near_call(reach, split, own, near, [0, 4, 1, 5], scale)
-    far = [first_four, second_four, first_eight, second_eight]
-    result = far_call(
-        reach, split, state, far, [2, 6, 3, 7], scale
-    )
+    near = [first_one, first_two, second_two]
+    state = near_call(reach, split, own, near, [0, 1, 5], scale)
+    far = [second_one, first_four, second_four, first_eight, second_eight]
+    result = far_call(reach, split, state, far, [4, 2, 6, 3, 7], scale)
     result = lax.all_to_all(result, "space", 0, 0, tiled=True)
     return jnp.transpose(result, (1, 0, 2)).reshape(1, rows, feat)
 

time: 97.5 us -> 94.6 us (0.970)
  blocking collectives: 41.4 us -> 35.5 us
  starting transfers between devices: 37.1 us -> 39.8 us
    all_to_all x1, blocking collectives: 17.1 us -> 11.2 us  [heads_plan(): result = lax.all_to_all(result, 'space', 0, 0, tiled=True)]
    all_to_all x1, waiting for transfers between devices: 0.01 us -> 4.73 us  [heads_plan(): split = lax.all_to_all(split, 'space', 0, 0, tiled=True)]
    ppermute x8, waiting for transfers between devices: 8.1 us -> 3.72 us  [crossed(): return lax.ppermute(array, 'frame', pairs)]
    ppermute x8, starting transfers between devices: 33.7 us -> 36.4 us  [crossed(): return lax.ppermute(array, 'frame', pairs)]
where the time goes in v5:
time: 94.6 us; the launch traced here: 93.9 us
  starting transfers between devices  39.8 us (42%)
  blocking collectives  35.5 us (38%)
  waiting for transfers between devices  8.45 us (9%)
  Pallas kernels  6.94 us (7%)
  local copies, waits for them, and re-layouts  1.81 us (2%)
  other arithmetic  1.15 us (1%)
    ppermute x8, starting transfers between devices, crossed(): return lax.ppermute(array, 'frame', pairs)  36.4 us
    all_to_all x1, blocking collectives, heads_plan(): lax.all_to_all(jnp.transpose(pair, (2, 0, 1, 3)), 'space', 0, 0, tiled=True)  24.3 us
    all_to_all x1, blocking collectives, heads_plan(): result = lax.all_to_all(result, 'space', 0, 0, tiled=True)  11.2 us
    all_to_all x1, waiting for transfers between devices, heads_plan(): split = lax.all_to_all(split, 'space', 0, 0, tiled=True)  4.73 us
    pallas_call x1, Pallas kernels, near_call(): pl.pallas_call(functools.partial(near_kernel, space * rows, columns, scal...  4.33 us
    ppermute x8, waiting for transfers between devices, crossed(): return lax.ppermute(array, 'frame', pairs)  3.72 us
    all_to_all x1, starting transfers between devices, heads_plan(): split = lax.all_to_all(split, 'space', 0, 0, tiled=True)  3.39 us
    pallas_call x1, Pallas kernels, far_call(): pl.pallas_call(functools.partial(far_kernel, space * rows, columns, scale...  2.61 us
  transfers between devices with their start and end apart: 9, of which 2 were waited for; matrix products, arithmetic and copies ran while one was open for 1% of the time, Pallas kernels for 5%

profile of v5, /device:TPU:1, one launch (start us, length us, event | category | flops | bytes accessed | tf_op | source)
XLA Modules:
  0.0 93.9 jit_solution(7233676810365330281)
XLA Ops:
  0.0 1.1 %pad_maximum_fusion = bf16[2,32,3072]{2,1,0:T(8,128)(2,1)S(1)} fusion(bf16[1,32,3072]{2,1,0:T(8,128)(2,1)} %param.6, bf16[1,32,3072]{2,1,0:T(8,128)(2,1)} %param.5), kind=kLoop, calls=%fused_computation.1 | loop fusion | flops 196608 | bytes 786432 | tf_op jit(solution)/shard_map/stack | solution.py:208
  1.1 0.0 copy-start
  1.1 24.3 %all_to_all.15.own = bf16[8,2,32,384]{3,2,1,0:T(8,128)(2,1)S(1)} all-to-all(bf16[8,2,32,384]{3,2,1,0:T(8,128)(2,1)S(1)} %bitcast.26), channel_id=1, replica_groups=mesh['frame'=64,'space'=8] {'space'}, dimensions={0} | all-to-all | bytes 786432 | tf_op jit(solution)/shard_map/all_to_all | solution.py:209
  25.4 1.3 %collective-permute-start = (bf16[8,2,32,384]{3,2,1,0:T(8,128)(2,1)S(1)}, bf16[8,2,32,384]{3,2,1,0:T(8,128)(2,1)S(1)}, u32[]{:S(2)}, u32[]{:S(2)}) collective-permute-start(bf16[8,2,32,384]{3,2,1,0:T(8,128)(2,1)S(1)} %all_to_all.15.own), channel_id=1, source_target_pairs={{0,16},{16,32},{24,8},{32,48},{40,24},{48,64},{56,40},{64,80},{72,... | collective-permute-start | bytes 1179656 | tf_op jit(solution)/shard_map/ppermute | solution.py:29
  26.7 4.0 %collective-permute-start.1 = (bf16[8,2,32,384]{3,2,1,0:T(8,128)(2,1)S(1)}, bf16[8,2,32,384]{3,2,1,0:T(8,128)(2,1)S(1)}, u32[]{:S(2)}, u32[]{:S(2)}) collective-permute-start(bf16[8,2,32,384]{3,2,1,0:T(8,128)(2,1)S(1)} %all_to_all.15.own), channel_id=1, source_target_pairs={{8,24},{16,0},{24,40},{32,16},{40,56},{48,32},{56,72},{64,48},{72,... | collective-permute-start | bytes 1179656 | tf_op jit(solution)/shard_map/ppermute | solution.py:29
  30.7 9.6 %collective-permute-start.6 = (bf16[8,2,32,384]{3,2,1,0:T(8,128)(2,1)S(1)}, bf16[8,2,32,384]{3,2,1,0:T(8,128)(2,1)S(1)}, u32[]{:S(2)}, u32[]{:S(2)}) collective-permute-start(bf16[8,2,32,384]{3,2,1,0:T(8,128)(2,1)S(1)} %all_to_all.15.own), channel_id=1, source_target_pairs={{0,64},{8,456},{16,80},{24,472},{32,96},{40,488},{48,112},{56,504}... | collective-permute-start | bytes 1179656 | tf_op jit(solution)/shard_map/ppermute | solution.py:29
  40.4 0.0 copy-done
  40.4 0.7 copy.13
  41.1 3.4 %all-to-all-start.1 = ((bf16[8,32,384]{2,1,0:T(8,128)(2,1)}), bf16[8,32,384]{2,1,0:T(8,128)(2,1)S(1)}, u32[]{:S(2)}, u32[]{:S(2)}) async-start(bf16[8,32,384]{2,1,0:T(8,128)(2,1)} %bitcast.25), calls=%async_computation.1 | async-start | bytes 393216 | tf_op jit(solution)/shard_map/all_to_all | solution.py:216
  44.5 0.0 copy-start.1
  44.5 3.9 %collective-permute-start.2 = (bf16[8,2,32,384]{3,2,1,0:T(8,128)(2,1)S(1)}, bf16[8,2,32,384]{3,2,1,0:T(8,128)(2,1)S(1)}, u32[]{:S(2)}, u32[]{:S(2)}) collective-permute-start(bf16[8,2,32,384]{3,2,1,0:T(8,128)(2,1)S(1)} %all_to_all.15.own), channel_id=1, source_target_pairs={{0,8},{8,0},{16,24},{24,16},{32,40},{40,32},{48,56},{56,48},{64,72... | collective-permute-start | bytes 1179656 | tf_op jit(solution)/shard_map/ppermute | solution.py:29
  48.4 0.0 copy-done.1
  48.5 0.1 slice.6
  48.5 0.1 slice.7
  48.6 4.7 %all-to-all-done.1.queries = bf16[8,32,384]{2,1,0:T(8,128)(2,1)S(1)} async-done(((bf16[8,32,384]{2,1,0:T(8,128)(2,1)}), bf16[8,32,384]{2,1,0:T(8,128)(2,1)S(1)}, u32[]{:S(2)}, u32[]{:S(2)}) %all-to-all-start.1) | async-done | bytes 196640 | tf_op jit(solution)/shard_map/all_to_all | solution.py:216
  53.4 0.0 collective-permute-done.refs_1_
  53.4 0.0 collective-permute-done.1.refs_2_
  53.4 1.3 %collective-permute-start.4 = (bf16[8,2,32,384]{3,2,1,0:T(8,128)(2,1)S(1)}, bf16[8,2,32,384]{3,2,1,0:T(8,128)(2,1)S(1)}, u32[]{:S(2)}, u32[]{:S(2)}) collective-permute-start(bf16[8,2,32,384]{3,2,1,0:T(8,128)(2,1)S(1)} %collective-permute-done.refs_1_), channel_id=1, source_target_pairs={{0,16},{16,32},{24,8},{32,48},{40,24},{48,64},{56,40},{64,80},{72,... | collective-permute-start | bytes 1179656 | tf_op jit(solution)/shard_map/ppermute | solution.py:29
  54.7 6.0 %collective-permute-start.3 = (bf16[8,2,32,384]{3,2,1,0:T(8,128)(2,1)S(1)}, bf16[8,2,32,384]{3,2,1,0:T(8,128)(2,1)S(1)}, u32[]{:S(2)}, u32[]{:S(2)}) collective-permute-start(bf16[8,2,32,384]{3,2,1,0:T(8,128)(2,1)S(1)} %all_to_all.15.own), channel_id=1, source_target_pairs={{8,16},{16,8},{24,32},{32,24},{40,48},{48,40},{56,64},{64,56},{72,... | collective-permute-start | bytes 1179656 | tf_op jit(solution)/shard_map/ppermute | solution.py:29
  60.7 8.3 %collective-permute-start.5 = (bf16[8,2,32,384]{3,2,1,0:T(8,128)(2,1)S(1)}, bf16[8,2,32,384]{3,2,1,0:T(8,128)(2,1)S(1)}, u32[]{:S(2)}, u32[]{:S(2)}) collective-permute-start(bf16[8,2,32,384]{3,2,1,0:T(8,128)(2,1)S(1)} %collective-permute-done.1.refs_2_), channel_id=1, source_target_pairs={{8,24},{16,0},{24,40},{32,16},{40,56},{48,32},{56,72},{64,48},{72,... | collective-permute-start | bytes 1179656 | tf_op jit(solution)/shard_map/ppermute | solution.py:29
  69.0 0.0 collective-permute-done.6.refs_3_
  69.0 2.0 %collective-permute-start.7 = (bf16[8,2,32,384]{3,2,1,0:T(8,128)(2,1)S(1)}, bf16[8,2,32,384]{3,2,1,0:T(8,128)(2,1)S(1)}, u32[]{:S(2)}, u32[]{:S(2)}) collective-permute-start(bf16[8,2,32,384]{3,2,1,0:T(8,128)(2,1)S(1)} %collective-permute-done.6.refs_3_), channel_id=1, source_target_pairs={{0,384},{8,136},{16,400},{24,152},{32,416},{40,168},{48,432},{56,1... | collective-permute-start | bytes 1179656 | tf_op jit(solution)/shard_map/ppermute | solution.py:29
  71.1 0.1 pad_add_fusion.reach
  71.1 0.0 collective-permute-done.2.refs_0_
  71.2 4.3 %own_and_near.1 = (f32[3,256,128]{2,1,0:T(8,128)S(1)}, f32[3,256,128]{2,1,0:T(8,128)S(1)}, f32[3,256,128]{2,1,0:T(8,128)S(1)}) custom-call(s32[8]{0:T(128)S(1)} %pad_add_fusion.reach, bf16[8,32,384]{2,1,0:T(8,128)(2,1)S(1)} %all-to-all-done.1.queries, bf16[8,2,32,384]{3,2,1,0:T(8,128)(2,1)S(1)} %all_to_all.15.own, ...), custom_call_target="tpu_custom_call" | custom-call | flops 1000000000 | bytes 6000000 | tf_op jit(solution)/shard_map/own_and_near/pallas_call | solution.py:165
  75.5 0.0 collective-permute-done.3.refs_0_
  75.5 0.0 collective-permute-done.4.refs_1_
  75.5 0.0 collective-permute-done.5.refs_2_
  75.5 3.7 %collective-permute-done.7.refs_4_ = bf16[8,2,32,384]{3,2,1,0:T(8,128)(2,1)S(1)} collective-permute-done((bf16[8,2,32,384]{3,2,1,0:T(8,128)(2,1)S(1)}, bf16[8,2,32,384]{3,2,1,0:T(8,128)(2,1)S(1)}, u32[]{:S(2)}, u32[]{:S(2)}) %collective-permute-start.7) | collective-permute-done | bytes 393248 | tf_op jit(solution)/shard_map/ppermute | solution.py:29
  79.2 2.6 %far_and_merge.1 = bf16[8,32,384]{2,1,0:T(8,128)(2,1)S(1)} custom-call(s32[8]{0:T(128)S(1)} %pad_add_fusion.reach, bf16[8,32,384]{2,1,0:T(8,128)(2,1)S(1)} %all-to-all-done.1.queries, f32[3,256,128]{2,1,0:T(8,128)S(1)} %get-tuple-element.15.top_in, f32[3,256,128]{2,1,0:T(8,128)S(1)} %get-tuple-element.16.sum_in, ...), custom_call_target="tpu_custom_call" | custom-call | flops 2000000000 | bytes 4000000 | tf_op jit(solution)/shard_map/far_and_merge/pallas_call | solution.py:181
  81.8 11.2 %all_to_all.16 = bf16[8,32,384]{2,1,0:T(8,128)(2,1)S(1)} all-to-all(bf16[8,32,384]{2,1,0:T(8,128)(2,1)S(1)} %far_and_merge.1), channel_id=1, replica_groups=mesh['frame'=64,'space'=8] {'space'}, dimensions={0} | all-to-all | bytes 393216 | tf_op jit(solution)/shard_map/all_to_all | solution.py:228
  93.0 0.1 copy.7
  93.1 0.8 reshape.7
  (3 shorter events, 0.1 us)
Async XLA Ops:
  1.1 39.3 %copy-start = (bf16[1,32,3072]{2,1,0:T(8,128)(2,1)S(1)}, bf16[1,32,3072]{2,1,0:T(8,128)(2,1)}, u32[]{:S(2)}) copy-start(bf16[1,32,3072]{2,1,0:T(8,128)(2,1)} %param.4) | copy-start | bytes 589828
  25.4 27.9 %collective-permute-start = (bf16[8,2,32,384]{3,2,1,0:T(8,128)(2,1)S(1)}, bf16[8,2,32,384]{3,2,1,0:T(8,128)(2,1)S(1)}, u32[]{:S(2)}, u32[]{:S(2)}) collective-permute-start(bf16[8,2,32,384]{3,2,1,0:T(8,128)(2,1)S(1)} %all_to_all.15.own), channel_id=1, source_target_pairs={{0,16},{16,32},{24,8},{32,48},{40,24},{48,64},{56,40},{64,80},{72,... | collective-permute-start | bytes 1179656 | tf_op jit(solution)/shard_map/ppermute | solution.py:29
  26.7 26.6 %collective-permute-start.1 = (bf16[8,2,32,384]{3,2,1,0:T(8,128)(2,1)S(1)}, bf16[8,2,32,384]{3,2,1,0:T(8,128)(2,1)S(1)}, u32[]{:S(2)}, u32[]{:S(2)}) collective-permute-start(bf16[8,2,32,384]{3,2,1,0:T(8,128)(2,1)S(1)} %all_to_all.15.own), channel_id=1, source_target_pairs={{8,24},{16,0},{24,40},{32,16},{40,56},{48,32},{56,72},{64,48},{72,... | collective-permute-start | bytes 1179656 | tf_op jit(solution)/shard_map/ppermute | solution.py:29
  30.7 38.3 %collective-permute-start.6 = (bf16[8,2,32,384]{3,2,1,0:T(8,128)(2,1)S(1)}, bf16[8,2,32,384]{3,2,1,0:T(8,128)(2,1)S(1)}, u32[]{:S(2)}, u32[]{:S(2)}) collective-permute-start(bf16[8,2,32,384]{3,2,1,0:T(8,128)(2,1)S(1)} %all_to_all.15.own), channel_id=1, source_target_pairs={{0,64},{8,456},{16,80},{24,472},{32,96},{40,488},{48,112},{56,504}... | collective-permute-start | bytes 1179656 | tf_op jit(solution)/shard_map/ppermute | solution.py:29
  41.1 12.2 %all-to-all-start.1 = ((bf16[8,32,384]{2,1,0:T(8,128)(2,1)}), bf16[8,32,384]{2,1,0:T(8,128)(2,1)S(1)}, u32[]{:S(2)}, u32[]{:S(2)}) async-start(bf16[8,32,384]{2,1,0:T(8,128)(2,1)} %bitcast.25), calls=%async_computation.1 | async-start | bytes 393216 | tf_op jit(solution)/shard_map/all_to_all | solution.py:216
  44.5 3.9 %copy-start.1 = (s32[1,8]{1,0:T(1,128)S(1)}, s32[1,8]{1,0:T(1,128)}, u32[]{:S(2)}) copy-start(s32[1,8]{1,0:T(1,128)} %param.7) | copy-start | bytes 100
  44.5 26.6 %collective-permute-start.2 = (bf16[8,2,32,384]{3,2,1,0:T(8,128)(2,1)S(1)}, bf16[8,2,32,384]{3,2,1,0:T(8,128)(2,1)S(1)}, u32[]{:S(2)}, u32[]{:S(2)}) collective-permute-start(bf16[8,2,32,384]{3,2,1,0:T(8,128)(2,1)S(1)} %all_to_all.15.own), channel_id=1, source_target_pairs={{0,8},{8,0},{16,24},{24,16},{32,40},{40,32},{48,56},{56,48},{64,72... | collective-permute-start | bytes 1179656 | tf_op jit(solution)/shard_map/ppermute | solution.py:29
  53.4 22.1 %collective-permute-start.4 = (bf16[8,2,32,384]{3,2,1,0:T(8,128)(2,1)S(1)}, bf16[8,2,32,384]{3,2,1,0:T(8,128)(2,1)S(1)}, u32[]{:S(2)}, u32[]{:S(2)}) collective-permute-start(bf16[8,2,32,384]{3,2,1,0:T(8,128)(2,1)S(1)} %collective-permute-done.refs_1_), channel_id=1, source_target_pairs={{0,16},{16,32},{24,8},{32,48},{40,24},{48,64},{56,40},{64,80},{72,... | collective-permute-start | bytes 1179656 | tf_op jit(solution)/shard_map/ppermute | solution.py:29
  54.7 20.8 %collective-permute-start.3 = (bf16[8,2,32,384]{3,2,1,0:T(8,128)(2,1)S(1)}, bf16[8,2,32,384]{3,2,1,0:T(8,128)(2,1)S(1)}, u32[]{:S(2)}, u32[]{:S(2)}) collective-permute-start(bf16[8,2,32,384]{3,2,1,0:T(8,128)(2,1)S(1)} %all_to_all.15.own), channel_id=1, source_target_pairs={{8,16},{16,8},{24,32},{32,24},{40,48},{48,40},{56,64},{64,56},{72,... | collective-permute-start | bytes 1179656 | tf_op jit(solution)/shard_map/ppermute | solution.py:29
  60.7 14.8 %collective-permute-start.5 = (bf16[8,2,32,384]{3,2,1,0:T(8,128)(2,1)S(1)}, bf16[8,2,32,384]{3,2,1,0:T(8,128)(2,1)S(1)}, u32[]{:S(2)}, u32[]{:S(2)}) collective-permute-start(bf16[8,2,32,384]{3,2,1,0:T(8,128)(2,1)S(1)} %collective-permute-done.1.refs_2_), channel_id=1, source_target_pairs={{8,24},{16,0},{24,40},{32,16},{40,56},{48,32},{56,72},{64,48},{72,... | collective-permute-start | bytes 1179656 | tf_op jit(solution)/shard_map/ppermute | solution.py:29
  69.0 10.2 %collective-permute-start.7 = (bf16[8,2,32,384]{3,2,1,0:T(8,128)(2,1)S(1)}, bf16[8,2,32,384]{3,2,1,0:T(8,128)(2,1)S(1)}, u32[]{:S(2)}, u32[]{:S(2)}) collective-permute-start(bf16[8,2,32,384]{3,2,1,0:T(8,128)(2,1)S(1)} %collective-permute-done.6.refs_3_), channel_id=1, source_target_pairs={{0,384},{8,136},{16,400},{24,152},{32,416},{40,168},{48,432},{56,1... | collective-permute-start | bytes 1179656 | tf_op jit(solution)/shard_map/ppermute | solution.py:29

commit v6 on v5

--- a/solution.py
+++ b/solution.py
@@ -216,7 +216,8 @@
     split = lax.all_to_all(split, "space", 0, 0, tiled=True)
     first_two, second_two, split = lax.optimization_barrier((first_two, second_two, split))
     first_four = crossed(first_two, 2, 1)
-    second_four = crossed(second_two, 2, -1)
+    second_two_late, first_eight = lax.optimization_barrier((second_two, first_eight))
+    second_four = crossed(second_two_late, 2, -1)
     own_late, _ = lax.optimization_barrier((own, first_two))
     second_one = crossed(own_late, 1, -1)
     second_eight = crossed(first_eight, 16, -1, has_other_far)

time: 94.6 us -> 95 us (level)
  waiting for transfers between devices: 8.45 us -> 10 us
  starting transfers between devices: 39.8 us -> 38.3 us
    ppermute x8, waiting for transfers between devices: 3.72 us -> 5.28 us  [crossed(): return lax.ppermute(array, 'frame', pairs)]
    ppermute x8, starting transfers between devices: 36.4 us -> 34.9 us  [crossed(): return lax.ppermute(array, 'frame', pairs)]
  transfers between devices with their start and end apart: 9 -> 9, of which waited for: 2 -> 3; matrix products, arithmetic and copies ran while one was open for 1% -> 1% of each run, Pallas kernels for 5% -> 5%
where the time goes in v6:
time: 95 us; the launch traced here: 94.4 us
  starting transfers between devices  38.3 us (40%)
  blocking collectives  36 us (38%)
  waiting for transfers between devices  10 us (11%)
  Pallas kernels  6.94 us (7%)
  local copies, waits for them, and re-layouts  1.81 us (2%)
  other arithmetic  1.15 us (1%)
    ppermute x8, starting transfers between devices, crossed(): return lax.ppermute(array, 'frame', pairs)  34.9 us
    all_to_all x1, blocking collectives, heads_plan(): lax.all_to_all(jnp.transpose(pair, (2, 0, 1, 3)), 'space', 0, 0, tiled=True)  24.3 us
    all_to_all x1, blocking collectives, heads_plan(): result = lax.all_to_all(result, 'space', 0, 0, tiled=True)  11.7 us
    ppermute x8, waiting for transfers between devices, crossed(): return lax.ppermute(array, 'frame', pairs)  5.28 us
    all_to_all x1, waiting for transfers between devices, heads_plan(): split = lax.all_to_all(split, 'space', 0, 0, tiled=True)  4.73 us
    pallas_call x1, Pallas kernels, near_call(): pl.pallas_call(functools.partial(near_kernel, space * rows, columns, scal...  4.33 us
    all_to_all x1, starting transfers between devices, heads_plan(): split = lax.all_to_all(split, 'space', 0, 0, tiled=True)  3.39 us
    pallas_call x1, Pallas kernels, far_call(): pl.pallas_call(functools.partial(far_kernel, space * rows, columns, scale...  2.61 us
  transfers between devices with their start and end apart: 9, of which 3 were waited for; matrix products, arithmetic and copies ran while one was open for 1% of the time, Pallas kernels for 5%

profile of v6, /device:TPU:1, one launch (start us, length us, event | category | flops | bytes accessed | tf_op | source)
XLA Modules:
  0.0 94.4 jit_solution(11083225328365511304)
XLA Ops:
  0.0 1.1 %pad_maximum_fusion = bf16[2,32,3072]{2,1,0:T(8,128)(2,1)S(1)} fusion(bf16[1,32,3072]{2,1,0:T(8,128)(2,1)} %param.6, bf16[1,32,3072]{2,1,0:T(8,128)(2,1)} %param.5), kind=kLoop, calls=%fused_computation.1 | loop fusion | flops 196608 | bytes 786432 | tf_op jit(solution)/shard_map/stack | solution.py:208
  1.1 0.0 copy-start
  1.1 24.3 %all_to_all.15.own = bf16[8,2,32,384]{3,2,1,0:T(8,128)(2,1)S(1)} all-to-all(bf16[8,2,32,384]{3,2,1,0:T(8,128)(2,1)S(1)} %bitcast.26), channel_id=1, replica_groups=mesh['frame'=64,'space'=8] {'space'}, dimensions={0} | all-to-all | bytes 786432 | tf_op jit(solution)/shard_map/all_to_all | solution.py:209
  25.4 1.3 %collective-permute-start = (bf16[8,2,32,384]{3,2,1,0:T(8,128)(2,1)S(1)}, bf16[8,2,32,384]{3,2,1,0:T(8,128)(2,1)S(1)}, u32[]{:S(2)}, u32[]{:S(2)}) collective-permute-start(bf16[8,2,32,384]{3,2,1,0:T(8,128)(2,1)S(1)} %all_to_all.15.own), channel_id=1, source_target_pairs={{0,16},{16,32},{24,8},{32,48},{40,24},{48,64},{56,40},{64,80},{72,... | collective-permute-start | bytes 1179656 | tf_op jit(solution)/shard_map/ppermute | solution.py:29
  26.7 4.0 %collective-permute-start.1 = (bf16[8,2,32,384]{3,2,1,0:T(8,128)(2,1)S(1)}, bf16[8,2,32,384]{3,2,1,0:T(8,128)(2,1)S(1)}, u32[]{:S(2)}, u32[]{:S(2)}) collective-permute-start(bf16[8,2,32,384]{3,2,1,0:T(8,128)(2,1)S(1)} %all_to_all.15.own), channel_id=1, source_target_pairs={{8,24},{16,0},{24,40},{32,16},{40,56},{48,32},{56,72},{64,48},{72,... | collective-permute-start | bytes 1179656 | tf_op jit(solution)/shard_map/ppermute | solution.py:29
  30.7 9.6 %collective-permute-start.5 = (bf16[8,2,32,384]{3,2,1,0:T(8,128)(2,1)S(1)}, bf16[8,2,32,384]{3,2,1,0:T(8,128)(2,1)S(1)}, u32[]{:S(2)}, u32[]{:S(2)}) collective-permute-start(bf16[8,2,32,384]{3,2,1,0:T(8,128)(2,1)S(1)} %all_to_all.15.own), channel_id=1, source_target_pairs={{0,64},{8,456},{16,80},{24,472},{32,96},{40,488},{48,112},{56,504}... | collective-permute-start | bytes 1179656 | tf_op jit(solution)/shard_map/ppermute | solution.py:29
  40.4 0.0 copy-done
  40.4 0.7 copy.13
  41.1 3.4 %all-to-all-start.1 = ((bf16[8,32,384]{2,1,0:T(8,128)(2,1)}), bf16[8,32,384]{2,1,0:T(8,128)(2,1)S(1)}, u32[]{:S(2)}, u32[]{:S(2)}) async-start(bf16[8,32,384]{2,1,0:T(8,128)(2,1)} %bitcast.25), calls=%async_computation.1 | async-start | bytes 393216 | tf_op jit(solution)/shard_map/all_to_all | solution.py:216
  44.5 0.0 copy-start.1
  44.5 3.9 %collective-permute-start.2 = (bf16[8,2,32,384]{3,2,1,0:T(8,128)(2,1)S(1)}, bf16[8,2,32,384]{3,2,1,0:T(8,128)(2,1)S(1)}, u32[]{:S(2)}, u32[]{:S(2)}) collective-permute-start(bf16[8,2,32,384]{3,2,1,0:T(8,128)(2,1)S(1)} %all_to_all.15.own), channel_id=1, source_target_pairs={{0,8},{8,0},{16,24},{24,16},{32,40},{40,32},{48,56},{56,48},{64,72... | collective-permute-start | bytes 1179656 | tf_op jit(solution)/shard_map/ppermute | solution.py:29
  48.4 0.0 copy-done.1
  48.5 0.1 slice.6
  48.5 0.1 slice.7
  48.6 4.7 %all-to-all-done.1.queries = bf16[8,32,384]{2,1,0:T(8,128)(2,1)S(1)} async-done(((bf16[8,32,384]{2,1,0:T(8,128)(2,1)}), bf16[8,32,384]{2,1,0:T(8,128)(2,1)S(1)}, u32[]{:S(2)}, u32[]{:S(2)}) %all-to-all-start.1) | async-done | bytes 196640 | tf_op jit(solution)/shard_map/all_to_all | solution.py:216
  53.4 0.0 collective-permute-done.refs_1_
  53.4 0.0 collective-permute-done.1.refs_2_
  53.4 1.3 %collective-permute-start.4 = (bf16[8,2,32,384]{3,2,1,0:T(8,128)(2,1)S(1)}, bf16[8,2,32,384]{3,2,1,0:T(8,128)(2,1)S(1)}, u32[]{:S(2)}, u32[]{:S(2)}) collective-permute-start(bf16[8,2,32,384]{3,2,1,0:T(8,128)(2,1)S(1)} %collective-permute-done.refs_1_), channel_id=1, source_target_pairs={{0,16},{16,32},{24,8},{32,48},{40,24},{48,64},{56,40},{64,80},{72,... | collective-permute-start | bytes 1179656 | tf_op jit(solution)/shard_map/ppermute | solution.py:29
  54.7 6.0 %collective-permute-start.3 = (bf16[8,2,32,384]{3,2,1,0:T(8,128)(2,1)S(1)}, bf16[8,2,32,384]{3,2,1,0:T(8,128)(2,1)S(1)}, u32[]{:S(2)}, u32[]{:S(2)}) collective-permute-start(bf16[8,2,32,384]{3,2,1,0:T(8,128)(2,1)S(1)} %all_to_all.15.own), channel_id=1, source_target_pairs={{8,16},{16,8},{24,32},{32,24},{40,48},{48,40},{56,64},{64,56},{72,... | collective-permute-start | bytes 1179656 | tf_op jit(solution)/shard_map/ppermute | solution.py:29
  60.7 1.6 %collective-permute-done.5.refs_3_ = bf16[8,2,32,384]{3,2,1,0:T(8,128)(2,1)S(1)} collective-permute-done((bf16[8,2,32,384]{3,2,1,0:T(8,128)(2,1)S(1)}, bf16[8,2,32,384]{3,2,1,0:T(8,128)(2,1)S(1)}, u32[]{:S(2)}, u32[]{:S(2)}) %collective-permute-start.5) | collective-permute-done | bytes 393248 | tf_op jit(solution)/shard_map/ppermute | solution.py:29
  62.2 6.8 %collective-permute-start.6 = (bf16[8,2,32,384]{3,2,1,0:T(8,128)(2,1)S(1)}, bf16[8,2,32,384]{3,2,1,0:T(8,128)(2,1)S(1)}, u32[]{:S(2)}, u32[]{:S(2)}) collective-permute-start(bf16[8,2,32,384]{3,2,1,0:T(8,128)(2,1)S(1)} %collective-permute-done.1.refs_2_), channel_id=1, source_target_pairs={{8,24},{16,0},{24,40},{32,16},{40,56},{48,32},{56,72},{64,48},{72,... | collective-permute-start | bytes 1179656 | tf_op jit(solution)/shard_map/ppermute | solution.py:29
  69.0 2.0 %collective-permute-start.7 = (bf16[8,2,32,384]{3,2,1,0:T(8,128)(2,1)S(1)}, bf16[8,2,32,384]{3,2,1,0:T(8,128)(2,1)S(1)}, u32[]{:S(2)}, u32[]{:S(2)}) collective-permute-start(bf16[8,2,32,384]{3,2,1,0:T(8,128)(2,1)S(1)} %collective-permute-done.5.refs_3_), channel_id=1, source_target_pairs={{0,384},{8,136},{16,400},{24,152},{32,416},{40,168},{48,432},{56,1... | collective-permute-start | bytes 1179656 | tf_op jit(solution)/shard_map/ppermute | solution.py:29
  71.1 0.1 pad_add_fusion.reach
  71.1 0.0 collective-permute-done.2.refs_0_
  71.2 4.3 %own_and_near.1 = (f32[3,256,128]{2,1,0:T(8,128)S(1)}, f32[3,256,128]{2,1,0:T(8,128)S(1)}, f32[3,256,128]{2,1,0:T(8,128)S(1)}) custom-call(s32[8]{0:T(128)S(1)} %pad_add_fusion.reach, bf16[8,32,384]{2,1,0:T(8,128)(2,1)S(1)} %all-to-all-done.1.queries, bf16[8,2,32,384]{3,2,1,0:T(8,128)(2,1)S(1)} %all_to_all.15.own, ...), custom_call_target="tpu_custom_call" | custom-call | flops 1000000000 | bytes 6000000 | tf_op jit(solution)/shard_map/own_and_near/pallas_call | solution.py:165
  75.5 0.0 collective-permute-done.3.refs_0_
  75.5 0.0 collective-permute-done.4.refs_1_
  75.5 0.0 collective-permute-done.6.refs_2_
  75.5 3.7 %collective-permute-done.7.refs_4_ = bf16[8,2,32,384]{3,2,1,0:T(8,128)(2,1)S(1)} collective-permute-done((bf16[8,2,32,384]{3,2,1,0:T(8,128)(2,1)S(1)}, bf16[8,2,32,384]{3,2,1,0:T(8,128)(2,1)S(1)}, u32[]{:S(2)}, u32[]{:S(2)}) %collective-permute-start.7) | collective-permute-done | bytes 393248 | tf_op jit(solution)/shard_map/ppermute | solution.py:29
  79.2 2.6 %far_and_merge.1 = bf16[8,32,384]{2,1,0:T(8,128)(2,1)S(1)} custom-call(s32[8]{0:T(128)S(1)} %pad_add_fusion.reach, bf16[8,32,384]{2,1,0:T(8,128)(2,1)S(1)} %all-to-all-done.1.queries, f32[3,256,128]{2,1,0:T(8,128)S(1)} %get-tuple-element.17.top_in, f32[3,256,128]{2,1,0:T(8,128)S(1)} %get-tuple-element.18.sum_in, ...), custom_call_target="tpu_custom_call" | custom-call | flops 2000000000 | bytes 4000000 | tf_op jit(solution)/shard_map/far_and_merge/pallas_call | solution.py:181
  81.8 11.7 %all_to_all.16 = bf16[8,32,384]{2,1,0:T(8,128)(2,1)S(1)} all-to-all(bf16[8,32,384]{2,1,0:T(8,128)(2,1)S(1)} %far_and_merge.1), channel_id=1, replica_groups=mesh['frame'=64,'space'=8] {'space'}, dimensions={0} | all-to-all | bytes 393216 | tf_op jit(solution)/shard_map/all_to_all | solution.py:229
  93.6 0.1 copy.7
  93.6 0.8 reshape.7
  (3 shorter events, 0.1 us)
Async XLA Ops:
  1.1 39.3 %copy-start = (bf16[1,32,3072]{2,1,0:T(8,128)(2,1)S(1)}, bf16[1,32,3072]{2,1,0:T(8,128)(2,1)}, u32[]{:S(2)}) copy-start(bf16[1,32,3072]{2,1,0:T(8,128)(2,1)} %param.4) | copy-start | bytes 589828
  25.4 27.9 %collective-permute-start = (bf16[8,2,32,384]{3,2,1,0:T(8,128)(2,1)S(1)}, bf16[8,2,32,384]{3,2,1,0:T(8,128)(2,1)S(1)}, u32[]{:S(2)}, u32[]{:S(2)}) collective-permute-start(bf16[8,2,32,384]{3,2,1,0:T(8,128)(2,1)S(1)} %all_to_all.15.own), channel_id=1, source_target_pairs={{0,16},{16,32},{24,8},{32,48},{40,24},{48,64},{56,40},{64,80},{72,... | collective-permute-start | bytes 1179656 | tf_op jit(solution)/shard_map/ppermute | solution.py:29
  26.7 26.6 %collective-permute-start.1 = (bf16[8,2,32,384]{3,2,1,0:T(8,128)(2,1)S(1)}, bf16[8,2,32,384]{3,2,1,0:T(8,128)(2,1)S(1)}, u32[]{:S(2)}, u32[]{:S(2)}) collective-permute-start(bf16[8,2,32,384]{3,2,1,0:T(8,128)(2,1)S(1)} %all_to_all.15.own), channel_id=1, source_target_pairs={{8,24},{16,0},{24,40},{32,16},{40,56},{48,32},{56,72},{64,48},{72,... | collective-permute-start | bytes 1179656 | tf_op jit(solution)/shard_map/ppermute | solution.py:29
  30.7 31.5 %collective-permute-start.5 = (bf16[8,2,32,384]{3,2,1,0:T(8,128)(2,1)S(1)}, bf16[8,2,32,384]{3,2,1,0:T(8,128)(2,1)S(1)}, u32[]{:S(2)}, u32[]{:S(2)}) collective-permute-start(bf16[8,2,32,384]{3,2,1,0:T(8,128)(2,1)S(1)} %all_to_all.15.own), channel_id=1, source_target_pairs={{0,64},{8,456},{16,80},{24,472},{32,96},{40,488},{48,112},{56,504}... | collective-permute-start | bytes 1179656 | tf_op jit(solution)/shard_map/ppermute | solution.py:29
  41.1 12.2 %all-to-all-start.1 = ((bf16[8,32,384]{2,1,0:T(8,128)(2,1)}), bf16[8,32,384]{2,1,0:T(8,128)(2,1)S(1)}, u32[]{:S(2)}, u32[]{:S(2)}) async-start(bf16[8,32,384]{2,1,0:T(8,128)(2,1)} %bitcast.25), calls=%async_computation.1 | async-start | bytes 393216 | tf_op jit(solution)/shard_map/all_to_all | solution.py:216
  44.5 3.9 %copy-start.1 = (s32[1,8]{1,0:T(1,128)S(1)}, s32[1,8]{1,0:T(1,128)}, u32[]{:S(2)}) copy-start(s32[1,8]{1,0:T(1,128)} %param.7) | copy-start | bytes 100
  44.5 26.6 %collective-permute-start.2 = (bf16[8,2,32,384]{3,2,1,0:T(8,128)(2,1)S(1)}, bf16[8,2,32,384]{3,2,1,0:T(8,128)(2,1)S(1)}, u32[]{:S(2)}, u32[]{:S(2)}) collective-permute-start(bf16[8,2,32,384]{3,2,1,0:T(8,128)(2,1)S(1)} %all_to_all.15.own), channel_id=1, source_target_pairs={{0,8},{8,0},{16,24},{24,16},{32,40},{40,32},{48,56},{56,48},{64,72... | collective-permute-start | bytes 1179656 | tf_op jit(solution)/shard_map/ppermute | solution.py:29
  53.4 22.1 %collective-permute-start.4 = (bf16[8,2,32,384]{3,2,1,0:T(8,128)(2,1)S(1)}, bf16[8,2,32,384]{3,2,1,0:T(8,128)(2,1)S(1)}, u32[]{:S(2)}, u32[]{:S(2)}) collective-permute-start(bf16[8,2,32,384]{3,2,1,0:T(8,128)(2,1)S(1)} %collective-permute-done.refs_1_), channel_id=1, source_target_pairs={{0,16},{16,32},{24,8},{32,48},{40,24},{48,64},{56,40},{64,80},{72,... | collective-permute-start | bytes 1179656 | tf_op jit(solution)/shard_map/ppermute | solution.py:29
  54.7 20.8 %collective-permute-start.3 = (bf16[8,2,32,384]{3,2,1,0:T(8,128)(2,1)S(1)}, bf16[8,2,32,384]{3,2,1,0:T(8,128)(2,1)S(1)}, u32[]{:S(2)}, u32[]{:S(2)}) collective-permute-start(bf16[8,2,32,384]{3,2,1,0:T(8,128)(2,1)S(1)} %all_to_all.15.own), channel_id=1, source_target_pairs={{8,16},{16,8},{24,32},{32,24},{40,48},{48,40},{56,64},{64,56},{72,... | collective-permute-start | bytes 1179656 | tf_op jit(solution)/shard_map/ppermute | solution.py:29
  62.2 13.3 %collective-permute-start.6 = (bf16[8,2,32,384]{3,2,1,0:T(8,128)(2,1)S(1)}, bf16[8,2,32,384]{3,2,1,0:T(8,128)(2,1)S(1)}, u32[]{:S(2)}, u32[]{:S(2)}) collective-permute-start(bf16[8,2,32,384]{3,2,1,0:T(8,128)(2,1)S(1)} %collective-permute-done.1.refs_2_), channel_id=1, source_target_pairs={{8,24},{16,0},{24,40},{32,16},{40,56},{48,32},{56,72},{64,48},{72,... | collective-permute-start | bytes 1179656 | tf_op jit(solution)/shard_map/ppermute | solution.py:29
  69.0 10.2 %collective-permute-start.7 = (bf16[8,2,32,384]{3,2,1,0:T(8,128)(2,1)S(1)}, bf16[8,2,32,384]{3,2,1,0:T(8,128)(2,1)S(1)}, u32[]{:S(2)}, u32[]{:S(2)}) collective-permute-start(bf16[8,2,32,384]{3,2,1,0:T(8,128)(2,1)S(1)} %collective-permute-done.5.refs_3_), channel_id=1, source_target_pairs={{0,384},{8,136},{16,400},{24,152},{32,416},{40,168},{48,432},{56,1... | collective-permute-start | bytes 1179656 | tf_op jit(solution)/shard_map/ppermute | solution.py:29
